TPU v7x, 32 devices: a whole 2x2x4 slice. The times are simulated.
32 devices in a mesh: ctx: 16 (over z, x, core), tp: 2 (over y).
Axes of the slice: x: 2, y: 2, z: 4, core: 2. Of those that a mesh axis runs over, the one named last changes fastest.
Arguments:
- features: bfloat16 [3, 2048, 8192], P(None, 'ctx', 'tp'), may hold values from -6 to 6
- conv_weight: float32 [3, 3, 8192], replicated, may hold values from -3 to 3
- decay_rates: float32 [16, 8192], P(None, ('tp', 'ctx')), may hold values from 1e-05 to 0.03
- residues: float32 [16, 8192], P(None, ('tp', 'ctx')), may hold values from -1.5 to 1.5
- skip_gain: float32 [8192], P(('tp', 'ctx')), may hold values from -1 to 1
- out_weight: bfloat16 [8192, 8192], P('tp', 'ctx'), may hold values from -0.0625 to 0.0625
Outputs:
- mixed: bfloat16 [2048, 8192], P('ctx', 'tp')
All inputs are finite; a program needn't handle non-finite values.
Results may differ from a plain program's by a relative error of at most 0.014.
Values may be sent and summed in bfloat16 or wider, within the bound.
No kernel may reach another device: no remote copies, remote signals or barrier semaphores. Data moves between devices by JAX's collectives and lax.ppermute only.
A program may use at most 192 MiB of HBM per device.

v0:
```python
import functools

import jax
import jax.numpy as jnp
from jax import lax
from jax.experimental import pallas as pl
from jax.experimental.pallas import tpu as pltpu
from jax.sharding import PartitionSpec as P

LANES = 128
SUBLANES = 8
GROUP = LANES * SUBLANES
HALO = 2
TAPS = 3
SIDE = 2
SLAB = SIDE * SIDE
F32 = jnp.float32
BF16 = jnp.bfloat16


def spread(scratch, halo, block, pitch):
    tokens = block.shape[0]
    for tile in range(SUBLANES):
        lanes = pl.ds(tile * LANES, LANES)
        scratch[pl.ds(tile * pitch + SUBLANES - HALO, HALO), :] = halo[:, lanes].astype(F32)
        scratch[pl.ds(tile * pitch + SUBLANES, tokens), :] = block[:, lanes].astype(F32)


def token(scratch, index, pitch):
    return scratch[pl.ds(index, SUBLANES, stride=pitch), :]


def tree_sum(terms):
    while len(terms) > 1:
        terms = [a + b for a, b in zip(terms[::2], terms[1::2])] + terms[len(terms) & ~1 :]
    return terms[0]


def filter_kernel(here, features, halo, taps, u_ref, query_ref, tap_rows, *rows):
    tokens = features.shape[1]
    pitch = tokens + SUBLANES
    for tile in range(SUBLANES):
        for which in range(3):
            for j in range(TAPS):
                row = which * TAPS + j
                tap_rows[row, tile : tile + 1] = taps[which, j : j + 1, tile * LANES : (tile + 1) * LANES]
    for which in range(3):
        spread(rows[which], halo.at[which], features.at[which], pitch)
    weights = [[tap_rows[which * TAPS + j] for j in range(TAPS)] for which in range(3)]

    def step(index, carry):
        carry = list(carry)
        for inner in range(SUBLANES):
            now = index * SUBLANES + inner
            filtered = []
            for which in range(3):
                last, before = carry[which]
                fresh = token(rows[which], now + SUBLANES, pitch)
                filtered.append(
                    weights[which][0] * fresh + weights[which][1] * last + weights[which][2] * before
                )
                carry[which] = (fresh, last)
            query_ref[0, now] = filtered[0]
            u_ref[0, now] = (filtered[1] * filtered[2]).astype(BF16).astype(F32)
        return tuple(carry)

    start = tuple(
        (token(rows[which], SUBLANES - 1, pitch), token(rows[which], SUBLANES - 2, pitch))
        for which in range(3)
    )
    lax.fori_loop(0, tokens // SUBLANES, step, start)


def registers(refs, rank, wide, first, count):
    pitch = wide.shape[0] // SUBLANES
    each = SUBLANES // SLAB
    for d in range(SLAB):
        for j in range(each):
            start = pl.multiple_of(((d ^ rank) * each + j) * pitch, SUBLANES)
            rows = refs[d][0, first : first + count, j * LANES : (j + 1) * LANES]
            wide[pl.ds(start, count), :] = rows.astype(F32)
    return [wide[pl.ds(m, SUBLANES, stride=pitch), :] for m in range(count)]


def state_kernel(modes, here, u_ref, *refs):
    rates, outs, wide = refs[:SLAB], refs[SLAB : 2 * SLAB], refs[-1]
    rank = here[1]
    tokens = u_ref.shape[1]
    decay = [jnp.exp(-rate) for rate in registers(rates, rank, wide, 0, modes)]

    def step(index, states):
        for inner in range(SUBLANES):
            u = u_ref[0, index * SUBLANES + inner]
            states = tuple(states[m] * decay[m] + u for m in range(modes))
        return states

    zero = tuple(jnp.zeros((SUBLANES, LANES), F32) for _ in range(modes))
    states = lax.fori_loop(0, tokens // SUBLANES, step, zero)
    each = SUBLANES // SLAB
    pitch = wide.shape[0] // SUBLANES
    for m in range(modes):
        wide[pl.ds(m, SUBLANES, stride=pitch), :] = states[m]
    for d in range(SLAB):
        for j in range(each):
            start = pl.multiple_of(((d ^ rank) * each + j) * pitch, SUBLANES)
            outs[d][0, :, j * LANES : (j + 1) * LANES] = wide[pl.ds(start, modes), :].astype(BF16)


def slab_kernel(tokens, here, rates, *refs):
    states, out = refs[:SLAB], refs[SLAB]
    slabs = rates.shape[0]
    for g in range(slabs):
        rate = rates[lax.rem(g - here[0] + slabs, slabs), : states[0].shape[1]]
        total = None
        for d in range(SLAB):
            later = (SLAB - 1 - (here[1] ^ d)).astype(F32) * float(tokens)
            term = jnp.exp(-later * rate) * states[d][g].astype(F32)
            total = term if total is None else total + term
        out[g] = total.astype(BF16)


def incoming_kernel(tokens, here, rates, *refs):
    slabs = rates.shape[0]
    states, earlier, outs = refs[:SLAB], refs[SLAB : SLAB + slabs - 1], refs[SLAB + slabs - 1 :]
    for g in range(slabs):
        rate = rates[lax.rem(g - here[0] + slabs, slabs), : states[0].shape[1]]
        entering = earlier[0][g].astype(F32)
        for k in range(1, slabs - 1):
            entering += jnp.exp(-float(k * SLAB * tokens) * rate) * earlier[k][g].astype(F32)
        for d in range(SLAB):
            block = here[1] ^ d
            total = jnp.exp(-(block.astype(F32) * float(tokens)) * rate) * entering
            for e in range(SLAB):
                if e != d:
                    between = block - 1 - (here[1] ^ e)
                    factor = jnp.exp(-(jnp.maximum(between, 0).astype(F32) * float(tokens)) * rate)
                    factor = jnp.where(between >= 0, factor, jnp.zeros_like(factor))
                    total += factor * states[e][g].astype(F32)
            outs[d][g] = total.astype(BF16)


def local_kernel(modes, here, u_ref, *refs):
    rates, y_ref, wide = refs[:SLAB], refs[-2], refs[-1]
    tokens = u_ref.shape[1]
    rate = registers(rates, here[1], wide, 0, modes)
    rest = registers(rates, here[1], wide, modes, modes + 1)
    decay = [jnp.exp(-r) for r in rate]
    weight = [rest[m] * jnp.sqrt(2.0 * rate[m]) for m in range(modes)]
    skip = rest[modes]

    def step(index, states):
        for inner in range(SUBLANES):
            now = index * SUBLANES + inner
            u = u_ref[0, now]
            states = tuple(states[m] * decay[m] + u for m in range(modes))
            y_ref[0, now] = tree_sum([weight[m] * states[m] for m in range(modes)] + [skip * u])
        return states

    zero = tuple(jnp.zeros((SUBLANES, LANES), F32) for _ in range(modes))
    lax.fori_loop(0, tokens // SUBLANES, step, zero)


def gated_kernel(modes, here, query_ref, y_ref, *refs):
    rates, incoming = refs[:SLAB], refs[SLAB : 2 * SLAB]
    out_ref, wide, out_rows = refs[2 * SLAB :]
    tokens = query_ref.shape[1]
    pitch = tokens + SUBLANES
    rate = registers(rates, here[1], wide, 0, modes)
    rest = registers(rates, here[1], wide, modes, modes)
    state = registers(incoming, here[1], wide, 0, modes)
    decay = [jnp.exp(-r) for r in rate]
    weighted = tuple(rest[m] * jnp.sqrt(2.0 * rate[m]) * state[m] for m in range(modes))

    def step(index, weighted):
        for inner in range(SUBLANES):
            now = index * SUBLANES + inner
            weighted = tuple(weighted[m] * decay[m] for m in range(modes))
            long_out = tree_sum([y_ref[0, now], *weighted])
            long_out = long_out.astype(BF16).astype(F32)
            out_rows[pl.ds(now, SUBLANES, stride=pitch), :] = query_ref[0, now] * long_out
        return weighted

    lax.fori_loop(0, tokens // SUBLANES, step, weighted)
    for tile in range(SUBLANES):
        out_ref[:, pl.ds(tile * LANES, LANES)] = out_rows[pl.ds(tile * pitch, tokens), :].astype(BF16)


def project_kernel(count, here, *refs):
    out_ref, slots, sems = refs[-3:]
    pieces, depth, share = slots.shape
    blocks, sources = refs[: SIDE * count], refs[SIDE * count : -3]
    half = depth // SIDE
    columns = pl.ds(pl.multiple_of(here[0] * share, share), share)
    copies = []
    for i in range(pieces):
        if len(sources) == pieces:
            source = sources[i].at[:, columns]
        else:
            source = sources[0].at[here[1 + i], :, columns]
        copies.append(pltpu.make_async_copy(source, slots.at[i], sems.at[i]))
        copies[-1].start()
    for i in range(pieces):
        copies[i].wait()
        for j in range(count):
            total = None
            for h in range(SIDE):
                term = jnp.dot(
                    blocks[SIDE * j + h][...],
                    slots[i, h * half : (h + 1) * half],
                    preferred_element_type=F32,
                )
                total = term if total is None else total + term
            out_ref[j, i] = total.astype(BF16)


def place_kernel(kept, steps, here, *refs):
    per_pair = 2 * steps
    sources, out_ref, sems = refs[: SIDE * per_pair], refs[-2], refs[-1]
    share = sources[0].shape[2]
    tp_me, rank = here[0], here[1]
    waits = []
    for slot in range(kept):
        step = here[2 + slot]
        for pair in range(SIDE):
            mine = sources[pair * per_pair : (pair + 1) * per_pair]
            for near in range(SIDE):
                piece = rank ^ (SIDE * pair + near)
                for t in range(SIDE):
                    start = ((slot * SLAB + piece) * SIDE + t) * share
                    target = out_ref.at[:, pl.ds(pl.multiple_of(start, share), share)]
                    sem = sems.at[len(waits)]
                    own = jnp.logical_and(step == 0, tp_me == t)
                    moved = jnp.logical_and(step == 0, tp_me != t)
                    choices = [(own, mine[0]), (moved, mine[1])]
                    choices += [(step == k, mine[2 * k + t]) for k in range(1, steps)]
                    for chosen, source in choices:
                        copy = pltpu.make_async_copy(source.at[near], target, sem)
                        pl.when(chosen)(copy.start)
                    waits.append(copy)
    for copy in waits:
        copy.wait()


def ring_order(count):
    return [0] + list(range(1, count, 2)) + [i for i in range(count - 1, 0, -1) if i % 2 == 0]


def any_size(features, conv_weight, decay_rates, residues, skip_gain, out_weight):
    tokens, width = features.shape[1:]
    ctx, tp = lax.axis_size("ctx"), lax.axis_size("tp")
    me, tp_me = lax.axis_index("ctx"), lax.axis_index("tp")
    halo = lax.ppermute(features[:, tokens - HALO :], "ctx", [(i, i + 1) for i in range(ctx - 1)])
    extended = jnp.concatenate([halo, features], axis=1).astype(F32)
    taps = lax.dynamic_slice_in_dim(conv_weight, tp_me * width, width, 2)
    filtered = sum(taps[:, j, None] * extended[:, HALO - j : HALO - j + tokens] for j in range(TAPS))
    u = (filtered[1] * filtered[2]).astype(BF16).astype(F32)
    rates, weights, skip = (
        lax.all_gather(a, "ctx", axis=a.ndim - 1, tiled=True) for a in (decay_rates, residues, skip_gain)
    )
    weights = weights * jnp.sqrt(2.0 * rates)
    decay = jnp.exp(-rates)
    zero = jnp.zeros(rates.shape, F32)
    left = lax.fori_loop(0, tokens, lambda t, s: s * decay + u[t], zero)
    lefts = lax.all_gather(left, "ctx")
    block_decay = jnp.exp(-float(tokens) * rates)
    entering = lax.fori_loop(0, me, lambda b, s: s * block_decay + lefts[b], zero)

    def advance(states, now):
        states = states * decay + now
        return states, jnp.sum(weights * states, axis=0) + skip * now

    long_out = lax.scan(advance, entering, u)[1].astype(BF16).astype(F32)
    gated = (filtered[0] * long_out).astype(BF16)
    whole = lax.all_gather(gated, "ctx", axis=0, tiled=True)
    partial = jnp.dot(whole, out_weight, preferred_element_type=F32).astype(BF16)
    share = partial.shape[1] // tp
    partial = partial.reshape(ctx * tokens, tp, share).transpose(1, 0, 2)
    partial = lax.all_to_all(partial, "tp", split_axis=0, concat_axis=0, tiled=True)
    summed = jnp.sum(partial.astype(F32), axis=0).astype(BF16).reshape(ctx, tokens, share)
    summed = lax.all_to_all(summed, "ctx", split_axis=0, concat_axis=0, tiled=True)
    placed = lax.all_to_all(
        summed.reshape(tp, ctx // tp, tokens, share), "tp", split_axis=0, concat_axis=0, tiled=True
    )
    return placed.transpose(2, 1, 0, 3).reshape(tokens, width)


def per_device(features, conv_weight, decay_rates, residues, skip_gain, out_weight):
    tokens, width = features.shape[1:]
    modes, owned = decay_rates.shape
    ctx, tp = lax.axis_size("ctx"), lax.axis_size("tp")
    depth, columns = out_weight.shape
    share = columns // tp
    if owned * SLAB != GROUP or tp != SIDE or share % LANES or ctx // SLAB < 3:
        return any_size(features, conv_weight, decay_rates, residues, skip_gain, out_weight)
    slabs = ctx // SLAB
    groups = width // GROUP
    me, tp_me = lax.axis_index("ctx"), lax.axis_index("tp")
    z_me, rank = me // SLAB, me % SLAB
    order = ring_order(slabs)
    place = [order.index(z) for z in range(slabs)]
    here = jnp.stack([z_me, rank, tp_me]).astype(jnp.int32)

    def within_slab(array, mask):
        return lax.ppermute(array, "ctx", [(i, i ^ mask) for i in range(ctx)])

    def slab_all(array):
        return [array] + [within_slab(array, mask) for mask in range(1, SLAB)]

    def from_slab(array, by):
        return lax.ppermute(array, "ctx", [(i, (i - by * SLAB) % ctx) for i in range(ctx)])

    def ring(array):
        pairs = []
        for i in range(ctx):
            z, rest = divmod(i, SLAB)
            pairs.append((i, order[(place[z] + 1) % slabs] * SLAB + rest))
        return lax.ppermute(array, "ctx", pairs)

    halo = lax.ppermute(
        features[:, tokens - HALO :, :], "ctx", [(i, i + 1) for i in range(ctx - 1)]
    )
    rows = jnp.concatenate([decay_rates, residues, skip_gain[None]], axis=0)
    rows = jnp.stack([rows] + [from_slab(rows, by) for by in range(1, slabs)])
    rates = slab_all(rows)

    beside = within_slab(out_weight, 1)
    slab_weights = lax.all_gather(
        out_weight,
        "ctx",
        axis_index_groups=[list(range(z * SLAB, (z + 1) * SLAB)) for z in range(slabs)],
    )

    limit = pltpu.CompilerParams(vmem_limit_bytes=16 * 1024 * 1024)
    series_shape = jax.ShapeDtypeStruct((groups, tokens, SUBLANES, LANES), F32)
    state_shape = jax.ShapeDtypeStruct((groups, modes, owned), BF16)
    scratch_rows = pltpu.VMEM((SUBLANES * (tokens + SUBLANES), LANES), F32)
    wide = pltpu.VMEM((SUBLANES * (modes + SUBLANES), LANES), F32)
    series = pl.BlockSpec((1, tokens, SUBLANES, LANES), lambda g, here: (g, 0, 0, 0))
    state_spec = pl.BlockSpec((1, modes, owned), lambda g, here: (g, 0, 0))
    rate_spec = pl.BlockSpec(
        (1, 2 * modes + 1, owned), lambda g, here: (lax.rem(g - here[0] + slabs, slabs), 0, 0)
    )

    def grouped(kernel, name, in_specs, out_specs, out_shape, scratch, ops, groups=groups):
        return pl.pallas_call(
            kernel,
            grid_spec=pltpu.PrefetchScalarGridSpec(
                num_scalar_prefetch=1,
                grid=(groups,),
                in_specs=in_specs,
                out_specs=out_specs,
                scratch_shapes=scratch,
            ),
            out_shape=out_shape,
            compiler_params=limit,
            cost_estimate=pl.CostEstimate(
                flops=ops * tokens * GROUP * groups,
                bytes_accessed=4 * tokens * GROUP * groups,
                transcendentals=0,
            ),
            name=name,
        )

    u, query = grouped(
        filter_kernel,
        "short_filters",
        [
            pl.BlockSpec((3, tokens, GROUP), lambda g, here: (0, 0, g)),
            pl.BlockSpec((3, HALO, GROUP), lambda g, here: (0, 0, g)),
            pl.BlockSpec((3, TAPS, GROUP), lambda g, here: (0, 0, here[2] * groups + g)),
        ],
        [series, series],
        [series_shape, series_shape],
        [pltpu.VMEM((3 * TAPS, SUBLANES, LANES), F32), scratch_rows, scratch_rows, scratch_rows],
        20,
    )(here, features, halo, conv_weight)

    left = grouped(
        functools.partial(state_kernel, modes),
        "block_states",
        [series] + [rate_spec] * SLAB,
        [state_spec] * SLAB,
        [state_shape] * SLAB,
        [wide],
        2 * modes,
    )(here, u, *rates)
    left = [left[0]] + [within_slab(left[d], d) for d in range(1, SLAB)]

    smem = pl.BlockSpec(memory_space=pltpu.SMEM)
    vmem = pl.BlockSpec(memory_space=pltpu.VMEM)
    slab_left = pl.pallas_call(
        functools.partial(slab_kernel, tokens),
        in_specs=[smem] + [vmem] * (1 + SLAB),
        out_specs=vmem,
        out_shape=state_shape,
        compiler_params=limit,
        name="slab_states",
    )(here, rows, *left)
    earlier = [
        lax.ppermute(slab_left, "ctx", [(i, i + by * SLAB) for i in range(ctx - by * SLAB)])
        for by in range(1, slabs)
    ]

    local = grouped(
        functools.partial(local_kernel, modes),
        "local_convolution",
        [series] + [rate_spec] * SLAB,
        series,
        series_shape,
        [wide],
        4 * modes,
    )(here, u, *rates)

    incoming = pl.pallas_call(
        functools.partial(incoming_kernel, tokens),
        in_specs=[smem] + [vmem] * (SLAB + slabs),
        out_specs=[vmem] * SLAB,
        out_shape=[state_shape] * SLAB,
        compiler_params=limit,
        name="incoming_states",
    )(here, rows, *left, *earlier)
    incoming = [incoming[0]] + [within_slab(incoming[d], d) for d in range(1, SLAB)]

    def gated_half(half):
        count = groups // SIDE
        first = half * count

        def shifted(spec):
            return pl.BlockSpec(spec.block_shape, lambda g, here: spec.index_map(g + first, here))

        return grouped(
            functools.partial(gated_kernel, modes),
            "gated_block",
            [shifted(s) for s in [series] * 2 + [rate_spec] * SLAB + [state_spec] * SLAB],
            pl.BlockSpec((tokens, GROUP), lambda g, here: (0, g)),
            jax.ShapeDtypeStruct((tokens, width // SIDE), BF16),
            [wide, scratch_rows],
            2 * modes,
            count,
        )(here, query, local, *rates, *incoming)

    def project(blocks, sources, share_index):
        scalars = jnp.stack([share_index, rank ^ 2, rank ^ 3]).astype(jnp.int32)
        rows = len(blocks) * tokens
        return pl.pallas_call(
            functools.partial(project_kernel, len(blocks)),
            in_specs=[smem]
            + [vmem] * (SIDE * len(blocks))
            + [pl.BlockSpec(memory_space=pltpu.HBM)] * len(sources),
            out_specs=vmem,
            out_shape=jax.ShapeDtypeStruct((len(blocks), SIDE, tokens, share), BF16),
            scratch_shapes=[
                pltpu.VMEM((SIDE, depth, share), BF16),
                pltpu.SemaphoreType.DMA((SIDE,)),
            ],
            compiler_params=pltpu.CompilerParams(vmem_limit_bytes=48 * 1024 * 1024),
            cost_estimate=pl.CostEstimate(
                flops=2 * rows * depth * SIDE * share,
                bytes_accessed=2 * depth * (rows + SIDE * share),
                transcendentals=0,
            ),
            name="project_block",
        )(scalars, *[h for b in blocks for h in b], *sources)

    def summed_over_tp(blocks, sources):
        away = project(blocks, sources, 1 - tp_me)
        got = lax.ppermute(away, "tp", [(0, 1), (1, 0)])
        mine = project(blocks, sources, tp_me)
        return (mine.astype(F32) + got.astype(F32)).astype(BF16)

    half_of = [z * tp // slabs for z in range(slabs)]

    def deliver(summed, by):
        pairs = [[], []]
        for i in range(ctx):
            z, rest = divmod(i, SLAB)
            target = order[(place[z] - by) % slabs] * SLAB + rest
            for t in range(tp):
                pairs[t].append((i * tp + t, target * tp + half_of[z]))
        if by == 0:
            moves = [p for p in pairs[0] + pairs[1] if p[0] != p[1]]
            return [summed, lax.ppermute(summed, ("ctx", "tp"), moves)]
        return [lax.ppermute(summed, ("ctx", "tp"), moves) for moves in pairs]

    blocks = [[gated_half(h) for h in range(SIDE)]]
    arrived = [[], []]
    for step in range(slabs):
        if step:
            blocks[step], summed, arrived[0] = lax.optimization_barrier(
                (blocks[step], summed, arrived[0])
            )
            arrived[0] += deliver(summed, step - 1)
        if step < slabs - 1:
            blocks.append([ring(h) for h in blocks[step]])
        summed = summed_over_tp([blocks[step]], [out_weight, beside])[0]
    arrived[0] += deliver(summed, slabs - 1)
    slab_weights, _ = lax.optimization_barrier((slab_weights, blocks[-1]))
    for first in range(0, slabs, 2):
        pair = summed_over_tp(blocks[first : first + 2], [slab_weights])
        for offset in range(pair.shape[0]):
            arrived[1] += deliver(pair[offset], first + offset)

    def place_of(z):
        return sum(jnp.where(z == k, place[k], 0) for k in range(slabs))

    kept = slabs // tp
    steps = [
        lax.rem(place_of(tp_me * kept + j) - place_of(z_me) + slabs, slabs) for j in range(kept)
    ]
    return pl.pallas_call(
        functools.partial(place_kernel, kept, slabs),
        in_specs=[smem] + [pl.BlockSpec(memory_space=pl.ANY)] * (SIDE * 2 * slabs),
        out_specs=pl.BlockSpec(memory_space=pl.ANY),
        out_shape=jax.ShapeDtypeStruct((tokens, width), BF16),
        scratch_shapes=[pltpu.SemaphoreType.DMA((kept * SLAB * SIDE,))],
        compiler_params=limit,
        name="place_columns",
    )(jnp.stack([tp_me, rank, *steps]).astype(jnp.int32), *arrived[0], *arrived[1])


def solution(mesh):
    in_specs = (
        P(None, "ctx", "tp"),
        P(),
        P(None, ("tp", "ctx")),
        P(None, ("tp", "ctx")),
        P(("tp", "ctx")),
        P("tp", "ctx"),
    )
    out_specs = P("ctx", "tp")
    return jax.shard_map(
        per_device, mesh=mesh, in_specs=in_specs, out_specs=out_specs, check_vma=False
    )
```

profile of v0, /device:TPU:4, one launch (start us, length us, event | category | flops | bytes accessed | tf_op | source)
XLA Modules:
  0.0 242.3 jit_solution(10220532442674561905)
XLA Ops:
  24.3 3.3 %short_filters.1 = (f32[4,128,8,128]{3,2,1,0:T(8,128)S(1)}, f32[4,128,8,128]{3,2,1,0:T(8,128)S(1)}) custom-call(s32[3]{0:T(128)S(1)} %pad_add_fusion.1.here, bf16[3,128,4096]{2,1,0:T(8,128)(2,1)S(1)} %copy-done.7, bf16[3,2,4096]{2,1,0:T(2,128)(2,1)S(1)} %collective-permute-done.halo, f32[3,3,8192]{2,1,0:T(4,128)S(1)} %copy-done.8), custom_call_target="tpu_custom_call" | custom-call | flops 10485760 | bytes 2097152 | tf_op jit(solution)/shard_map/short_filters/pallas_call | solution.py:364
  32.1 6.7 %collective-permute-start.7 = (bf16[4,16,256]{2,1,0:T(8,128)(2,1)S(1)}, bf16[4,16,256]{2,1,0:T(8,128)(2,1)S(1)}, u32[]{:S(2)}, u32[]{:S(2)}) collective-permute-start(bf16[4,16,256]{2,1,0:T(8,128)(2,1)S(1)} %get-tuple-element.34), channel_id=1, source_target_pairs={{0,2},{2,0},{4,6},{6,4},{8,10},{10,8},{12,14},{14,12},{16,18},{18,... | collective-permute-start | bytes 98312 | tf_op jit(solution)/shard_map/ppermute | solution.py:304
  48.1 5.1 %collective-permute-start.11 = (bf16[4,16,256]{2,1,0:T(8,128)(2,1)S(1)}, bf16[4,16,256]{2,1,0:T(8,128)(2,1)S(1)}, u32[]{:S(2)}, u32[]{:S(2)}) collective-permute-start(bf16[4,16,256]{2,1,0:T(8,128)(2,1)S(1)} %slab_states.1), channel_id=1, source_target_pairs={{0,16},{2,18},{4,20},{6,22},{8,24},{10,26},{12,28},{14,30},{1,17},... | collective-permute-start | bytes 98312 | tf_op jit(solution)/shard_map/ppermute | solution.py:400
  58.8 5.5 %local_convolution.1.y_ref = f32[4,128,8,128]{3,2,1,0:T(8,128)S(1)} custom-call(s32[3]{0:T(128)S(1)} %pad_add_fusion.1.here, f32[4,128,8,128]{3,2,1,0:T(8,128)S(1)} %get-tuple-element.32.u_ref, f32[4,33,256]{2,1,0:T(8,128)S(1)} %pad_maximum_fusion.refs_0_.rates, f32[4,33,256]{2,1,0:T(8,128)S(1)} %collective-permute-done.4.refs_1_, ...), custom_call_target="tpu_custom_call" | custom-call | flops 33554432 | bytes 2097152 | tf_op jit(solution)/shard_map/local_convolution/pallas_call | solution.py:404
  69.3 4.7 %collective-permute-start.17 = (bf16[128,2048]{1,0:T(8,128)(2,1)S(1)}, bf16[128,2048]{1,0:T(8,128)(2,1)S(1)}, u32[]{:S(2)}, u32[]{:S(2)}) collective-permute-start(bf16[128,2048]{1,0:T(8,128)(2,1)S(1)} %gated_block.3.refs_1_), channel_id=1, source_target_pairs={{0,8},{2,10},{4,12},{6,14},{8,24},{10,26},{12,28},{14,30},{16,0},{... | collective-permute-start | bytes 1572872 | tf_op jit(solution)/shard_map/ppermute | solution.py:317
  82.5 10.7 %collective-permute-done.17.refs_1_.refs_3_ = bf16[128,2048]{1,0:T(8,128)(2,1)S(1)} collective-permute-done((bf16[128,2048]{1,0:T(8,128)(2,1)S(1)}, bf16[128,2048]{1,0:T(8,128)(2,1)S(1)}, u32[]{:S(2)}, u32[]{:S(2)}) %collective-permute-start.17) | collective-permute-done | bytes 524320 | tf_op jit(solution)/shard_map/ppermute | solution.py:317
  94.5 3.4 %collective-permute-start.21 = (bf16[128,2048]{1,0:T(8,128)(2,1)S(1)}, bf16[128,2048]{1,0:T(8,128)(2,1)S(1)}, u32[]{:S(2)}, u32[]{:S(2)}) collective-permute-start(bf16[128,2048]{1,0:T(8,128)(2,1)S(1)} %collective-permute-done.17.refs_1_.refs_3_), channel_id=1, source_target_pairs={{0,8},{2,10},{4,12},{6,14},{8,24},{10,26},{12,28},{14,30},{16,0},{... | collective-permute-start | bytes 1572872 | tf_op jit(solution)/shard_map/ppermute | solution.py:317
  101.4 3.4 %collective-permute-start.23 = (bf16[2,128,256]{2,1,0:T(8,128)(2,1)S(1)}, bf16[2,128,256]{2,1,0:T(8,128)(2,1)S(1)}, u32[]{:S(2)}, u32[]{:S(2)}) collective-permute-start(bf16[2,128,256]{2,1,0:T(8,128)(2,1)S(1)} %fusion.refs_0_), channel_id=1, source_target_pairs={{16,17},{18,19},{20,21},{22,23},{24,25},{26,27},{28,29},{30,31},{1... | collective-permute-start | bytes 393224 | tf_op jit(solution)/shard_map/ppermute | solution.py:482
  108.9 9.8 %collective-permute-done.21.refs_1_ = bf16[128,2048]{1,0:T(8,128)(2,1)S(1)} collective-permute-done((bf16[128,2048]{1,0:T(8,128)(2,1)S(1)}, bf16[128,2048]{1,0:T(8,128)(2,1)S(1)}, u32[]{:S(2)}, u32[]{:S(2)}) %collective-permute-start.21) | collective-permute-done | bytes 524320 | tf_op jit(solution)/shard_map/ppermute | solution.py:317
  120.0 3.4 %collective-permute-start.25 = (bf16[128,2048]{1,0:T(8,128)(2,1)S(1)}, bf16[128,2048]{1,0:T(8,128)(2,1)S(1)}, u32[]{:S(2)}, u32[]{:S(2)}) collective-permute-start(bf16[128,2048]{1,0:T(8,128)(2,1)S(1)} %collective-permute-done.21.refs_1_), channel_id=1, source_target_pairs={{0,8},{2,10},{4,12},{6,14},{8,24},{10,26},{12,28},{14,30},{16,0},{... | collective-permute-start | bytes 1572872 | tf_op jit(solution)/shard_map/ppermute | solution.py:317
  127.6 4.3 %collective-permute-start.28 = (bf16[2,128,256]{2,1,0:T(8,128)(2,1)S(1)}, bf16[2,128,256]{2,1,0:T(8,128)(2,1)S(1)}, u32[]{:S(2)}, u32[]{:S(2)}) collective-permute-start(bf16[2,128,256]{2,1,0:T(8,128)(2,1)S(1)} %fusion.1), channel_id=1, source_target_pairs={{1,16},{3,18},{5,20},{7,22},{9,0},{11,2},{13,4},{15,6},{17,25},{19... | collective-permute-start | bytes 393224 | tf_op jit(solution)/shard_map/ppermute | solution.py:483
  135.6 8.5 %collective-permute-done.28.refs_3_ = bf16[2,128,256]{2,1,0:T(8,128)(2,1)S(1)} collective-permute-done((bf16[2,128,256]{2,1,0:T(8,128)(2,1)S(1)}, bf16[2,128,256]{2,1,0:T(8,128)(2,1)S(1)}, u32[]{:S(2)}, u32[]{:S(2)}) %collective-permute-start.28) | collective-permute-done | bytes 131104 | tf_op jit(solution)/shard_map/ppermute | solution.py:483
  147.1 3.6 %collective-permute-start.31 = (bf16[1,2,128,256]{3,2,1,0:T(8,128)(2,1)S(1)}, bf16[1,2,128,256]{3,2,1,0:T(8,128)(2,1)S(1)}, u32[]{:S(2)}, u32[]{:S(2)}) collective-permute-start(bf16[1,2,128,256]{3,2,1,0:T(8,128)(2,1)S(1)} %project_block.19), channel_id=1, source_target_pairs={{0,1},{1,0},{2,3},{3,2},{4,5},{5,4},{6,7},{7,6},{8,9},{9,8},{10,11... | collective-permute-start | bytes 393224 | tf_op jit(solution)/shard_map/ppermute | solution.py:467
  151.9 7.4 %collective-permute-start.30 = (bf16[2,128,256]{2,1,0:T(8,128)(2,1)}, bf16[2,128,256]{2,1,0:T(8,128)(2,1)}, u32[]{:S(2)}, u32[]{:S(2)}) collective-permute-start(bf16[2,128,256]{2,1,0:T(8,128)(2,1)} %fusion.2), channel_id=1, source_target_pairs={{1,24},{3,26},{5,28},{7,30},{9,16},{11,18},{13,20},{15,22},{17,9},... | collective-permute-start | bytes 393224 | tf_op jit(solution)/shard_map/ppermute | solution.py:483
  166.9 3.6 %project_block.21 = bf16[2,2,128,256]{3,2,1,0:T(8,128)(2,1)S(1)} custom-call(s32[3]{0:T(128)S(1)} %add_add_fusion.1.here, bf16[128,2048]{1,0:T(8,128)(2,1)S(1)} %gated_block.2.refs_0_, bf16[128,2048]{1,0:T(8,128)(2,1)S(1)} %gated_block.3.refs_1_, bf16[128,2048]{1,0:T(8,128)(2,1)S(1)} %collective-permute-done.16.refs_0_.refs_2_, ...), custom_call_target="tpu_custom_call" | custom-call | flops 1073741824 | bytes 6291456 | tf_op jit(solution)/shard_map/project_block/pallas_call | solution.py:445
  170.6 3.6 %project_block.20 = bf16[2,2,128,256]{3,2,1,0:T(8,128)(2,1)S(1)} custom-call(s32[3]{0:T(128)S(1)} %add_add_fusion.here, bf16[128,2048]{1,0:T(8,128)(2,1)S(1)} %gated_block.2.refs_0_, bf16[128,2048]{1,0:T(8,128)(2,1)S(1)} %gated_block.3.refs_1_, bf16[128,2048]{1,0:T(8,128)(2,1)S(1)} %collective-permute-done.16.refs_0_.refs_2_, ...), custom_call_target="tpu_custom_call" | custom-call | flops 1073741824 | bytes 6291456 | tf_op jit(solution)/shard_map/project_block/pallas_call | solution.py:445
  174.2 3.6 %project_block.23 = bf16[2,2,128,256]{3,2,1,0:T(8,128)(2,1)S(1)} custom-call(s32[3]{0:T(128)S(1)} %add_add_fusion.1.here, bf16[128,2048]{1,0:T(8,128)(2,1)S(1)} %collective-permute-done.20.refs_0_, bf16[128,2048]{1,0:T(8,128)(2,1)S(1)} %collective-permute-done.21.refs_1_, bf16[128,2048]{1,0:T(8,128)(2,1)S(1)} %copy-done.2, bf16[128,2048]{1,0:T(8,128)(2,1)S(1)} %copy-done.4, ...), custom_call_target="tpu_custom_call" | custom-call | flops 1073741824 | bytes 6291456 | tf_op jit(solution)/shard_map/project_block/pallas_call | solution.py:445
  177.9 3.6 %project_block.22 = bf16[2,2,128,256]{3,2,1,0:T(8,128)(2,1)S(1)} custom-call(s32[3]{0:T(128)S(1)} %add_add_fusion.here, bf16[128,2048]{1,0:T(8,128)(2,1)S(1)} %collective-permute-done.20.refs_0_, bf16[128,2048]{1,0:T(8,128)(2,1)S(1)} %collective-permute-done.21.refs_1_, bf16[128,2048]{1,0:T(8,128)(2,1)S(1)} %copy-done.2, bf16[128,2048]{1,0:T(8,128)(2,1)S(1)} %copy-done.4, ...), custom_call_target="tpu_custom_call" | custom-call | flops 1073741824 | bytes 6291456 | tf_op jit(solution)/shard_map/project_block/pallas_call | solution.py:445
  183.7 5.0 %collective-permute-done.38 = bf16[2,2,128,256]{3,2,1,0:T(8,128)(2,1)S(1)} collective-permute-done((bf16[2,2,128,256]{3,2,1,0:T(8,128)(2,1)S(1)}, bf16[2,2,128,256]{3,2,1,0:T(8,128)(2,1)S(1)}, u32[]{:S(2)}, u32[]{:S(2)}) %collective-permute-start.38) | collective-permute-done | bytes 262176 | tf_op jit(solution)/shard_map/ppermute | solution.py:467
  188.7 3.6 %collective-permute-start.35 = (bf16[2,128,256]{2,1,0:T(8,128)(2,1)S(1)}, bf16[2,128,256]{2,1,0:T(8,128)(2,1)S(1)}, u32[]{:S(2)}, u32[]{:S(2)}) collective-permute-start(bf16[2,128,256]{2,1,0:T(8,128)(2,1)S(1)} %get-tuple-element.60.refs_8_), channel_id=1, source_target_pairs={{16,17},{18,19},{20,21},{22,23},{24,25},{26,27},{28,29},{30,31},{1... | collective-permute-start | bytes 393224 | tf_op jit(solution)/shard_map/ppermute | solution.py:482
  193.1 7.0 %collective-permute-start.37 = (bf16[2,128,256]{2,1,0:T(8,128)(2,1)S(1)}, bf16[2,128,256]{2,1,0:T(8,128)(2,1)S(1)}, u32[]{:S(2)}, u32[]{:S(2)}) collective-permute-start(bf16[2,128,256]{2,1,0:T(8,128)(2,1)S(1)} %get-tuple-element.59), channel_id=1, source_target_pairs={{1,16},{3,18},{5,20},{7,22},{9,0},{11,2},{13,4},{15,6},{17,25},{19... | collective-permute-start | bytes 393224 | tf_op jit(solution)/shard_map/ppermute | solution.py:483
  201.5 7.2 %collective-permute-start.40 = (bf16[2,128,256]{2,1,0:T(8,128)(2,1)S(1)}, bf16[2,128,256]{2,1,0:T(8,128)(2,1)S(1)}, u32[]{:S(2)}, u32[]{:S(2)}) collective-permute-start(bf16[2,128,256]{2,1,0:T(8,128)(2,1)S(1)} %get-tuple-element.58), channel_id=1, source_target_pairs={{1,24},{3,26},{5,28},{7,30},{9,16},{11,18},{13,20},{15,22},{17,9},... | collective-permute-start | bytes 393224 | tf_op jit(solution)/shard_map/ppermute | solution.py:483
  212.7 4.7 %collective-permute-done.41.refs_14_ = bf16[2,128,256]{2,1,0:T(8,128)(2,1)S(1)} collective-permute-done((bf16[2,128,256]{2,1,0:T(8,128)(2,1)S(1)}, bf16[2,128,256]{2,1,0:T(8,128)(2,1)S(1)}, u32[]{:S(2)}, u32[]{:S(2)}) %collective-permute-start.41) | collective-permute-done | bytes 131104 | tf_op jit(solution)/shard_map/ppermute | solution.py:483
  217.8 17.7 %place_columns.1 = bf16[128,4096]{1,0:T(8,128)(2,1)} custom-call(s32[4]{0:T(128)S(1)} %pad_add_fusion.here, bf16[2,128,256]{2,1,0:T(8,128)(2,1)S(1)} %fusion.refs_0_, bf16[2,128,256]{2,1,0:T(8,128)(2,1)S(1)} %collective-permute-done.23.refs_1_, bf16[2,128,256]{2,1,0:T(8,128)(2,1)S(1)} %copy-done.10, bf16[2,128,256]{2,1,0:T(8,128)(2,1)S(1)} %copy-done.12, ...), custom_call_target="tpu_custom_call" | custom-call | tf_op jit(solution)/shard_map/place_columns/pallas_call | solution.py:510
  (132 shorter events, 88.7 us)
Async XLA Ops:
  6.5 160.3 %all-gather.3.cloned.1.call-start = ((), (), s32[]{:S(2)}) async-start(), calls=%async_computation | async-start | bytes 20971520 | tf_op jit(solution)/shard_map/all_gather | solution.py:327
  7.3 66.8 %collective-permute-start.18 = (bf16[4096,512]{1,0:T(8,128)(2,1)}, bf16[4096,512]{1,0:T(8,128)(2,1)}, u32[]{:S(2)}, u32[]{:S(2)}) collective-permute-start(bf16[4096,512]{1,0:T(8,128)(2,1)} %refs_2_.15), channel_id=1, source_target_pairs={{0,2},{2,0},{4,6},{6,4},{8,10},{10,8},{12,14},{14,12},{16,18},{18,... | collective-permute-start | bytes 12582920 | tf_op jit(solution)/shard_map/ppermute | solution.py:304
  15.7 13.3 %collective-permute-start.4 = (f32[4,33,256]{2,1,0:T(8,128)S(1)}, f32[4,33,256]{2,1,0:T(8,128)S(1)}, u32[]{:S(2)}, u32[]{:S(2)}) collective-permute-start(f32[4,33,256]{2,1,0:T(8,128)S(1)} %pad_maximum_fusion.refs_0_.rates), channel_id=1, source_target_pairs={{0,2},{2,0},{4,6},{6,4},{8,10},{10,8},{12,14},{14,12},{16,18},{18,... | collective-permute-start | bytes 405512 | tf_op jit(solution)/shard_map/ppermute | solution.py:304
  15.8 13.2 %collective-permute-start.5 = (f32[4,33,256]{2,1,0:T(8,128)S(1)}, f32[4,33,256]{2,1,0:T(8,128)S(1)}, u32[]{:S(2)}, u32[]{:S(2)}) collective-permute-start(f32[4,33,256]{2,1,0:T(8,128)S(1)} %pad_maximum_fusion.refs_0_.rates), channel_id=1, source_target_pairs={{0,4},{2,6},{4,0},{6,2},{8,12},{10,14},{12,8},{14,10},{16,20},{18,... | collective-permute-start | bytes 405512 | tf_op jit(solution)/shard_map/ppermute | solution.py:304
  17.3 11.7 %collective-permute-start.6 = (f32[4,33,256]{2,1,0:T(8,128)S(1)}, f32[4,33,256]{2,1,0:T(8,128)S(1)}, u32[]{:S(2)}, u32[]{:S(2)}) collective-permute-start(f32[4,33,256]{2,1,0:T(8,128)S(1)} %pad_maximum_fusion.refs_0_.rates), channel_id=1, source_target_pairs={{0,6},{2,4},{4,2},{6,0},{8,14},{10,12},{12,10},{14,8},{16,22},{18,... | collective-permute-start | bytes 405512 | tf_op jit(solution)/shard_map/ppermute | solution.py:304
  32.1 9.0 %collective-permute-start.7 = (bf16[4,16,256]{2,1,0:T(8,128)(2,1)S(1)}, bf16[4,16,256]{2,1,0:T(8,128)(2,1)S(1)}, u32[]{:S(2)}, u32[]{:S(2)}) collective-permute-start(bf16[4,16,256]{2,1,0:T(8,128)(2,1)S(1)} %get-tuple-element.34), channel_id=1, source_target_pairs={{0,2},{2,0},{4,6},{6,4},{8,10},{10,8},{12,14},{14,12},{16,18},{18,... | collective-permute-start | bytes 98312 | tf_op jit(solution)/shard_map/ppermute | solution.py:304
  66.8 15.7 %collective-permute-start.16 = (bf16[128,2048]{1,0:T(8,128)(2,1)S(1)}, bf16[128,2048]{1,0:T(8,128)(2,1)S(1)}, u32[]{:S(2)}, u32[]{:S(2)}) collective-permute-start(bf16[128,2048]{1,0:T(8,128)(2,1)S(1)} %gated_block.2.refs_0_), channel_id=1, source_target_pairs={{0,8},{2,10},{4,12},{6,14},{8,24},{10,26},{12,28},{14,30},{16,0},{... | collective-permute-start | bytes 1572872 | tf_op jit(solution)/shard_map/ppermute | solution.py:317
  69.3 23.9 %collective-permute-start.17 = (bf16[128,2048]{1,0:T(8,128)(2,1)S(1)}, bf16[128,2048]{1,0:T(8,128)(2,1)S(1)}, u32[]{:S(2)}, u32[]{:S(2)}) collective-permute-start(bf16[128,2048]{1,0:T(8,128)(2,1)S(1)} %gated_block.3.refs_1_), channel_id=1, source_target_pairs={{0,8},{2,10},{4,12},{6,14},{8,24},{10,26},{12,28},{14,30},{16,0},{... | collective-permute-start | bytes 1572872 | tf_op jit(solution)/shard_map/ppermute | solution.py:317
  93.2 15.7 %collective-permute-start.20 = (bf16[128,2048]{1,0:T(8,128)(2,1)S(1)}, bf16[128,2048]{1,0:T(8,128)(2,1)S(1)}, u32[]{:S(2)}, u32[]{:S(2)}) collective-permute-start(bf16[128,2048]{1,0:T(8,128)(2,1)S(1)} %collective-permute-done.16.refs_0_.refs_2_), channel_id=1, source_target_pairs={{0,8},{2,10},{4,12},{6,14},{8,24},{10,26},{12,28},{14,30},{16,0},{... | collective-permute-start | bytes 1572872 | tf_op jit(solution)/shard_map/ppermute | solution.py:317
  94.5 24.2 %collective-permute-start.21 = (bf16[128,2048]{1,0:T(8,128)(2,1)S(1)}, bf16[128,2048]{1,0:T(8,128)(2,1)S(1)}, u32[]{:S(2)}, u32[]{:S(2)}) collective-permute-start(bf16[128,2048]{1,0:T(8,128)(2,1)S(1)} %collective-permute-done.17.refs_1_.refs_3_), channel_id=1, source_target_pairs={{0,8},{2,10},{4,12},{6,14},{8,24},{10,26},{12,28},{14,30},{16,0},{... | collective-permute-start | bytes 1572872 | tf_op jit(solution)/shard_map/ppermute | solution.py:317
  118.7 25.4 %collective-permute-start.24 = (bf16[128,2048]{1,0:T(8,128)(2,1)S(1)}, bf16[128,2048]{1,0:T(8,128)(2,1)S(1)}, u32[]{:S(2)}, u32[]{:S(2)}) collective-permute-start(bf16[128,2048]{1,0:T(8,128)(2,1)S(1)} %collective-permute-done.20.refs_0_), channel_id=1, source_target_pairs={{0,8},{2,10},{4,12},{6,14},{8,24},{10,26},{12,28},{14,30},{16,0},{... | collective-permute-start | bytes 1572872 | tf_op jit(solution)/shard_map/ppermute | solution.py:317
  120.0 24.1 %collective-permute-start.25 = (bf16[128,2048]{1,0:T(8,128)(2,1)S(1)}, bf16[128,2048]{1,0:T(8,128)(2,1)S(1)}, u32[]{:S(2)}, u32[]{:S(2)}) collective-permute-start(bf16[128,2048]{1,0:T(8,128)(2,1)S(1)} %collective-permute-done.21.refs_1_), channel_id=1, source_target_pairs={{0,8},{2,10},{4,12},{6,14},{8,24},{10,26},{12,28},{14,30},{16,0},{... | collective-permute-start | bytes 1572872 | tf_op jit(solution)/shard_map/ppermute | solution.py:317
  127.6 16.5 %collective-permute-start.28 = (bf16[2,128,256]{2,1,0:T(8,128)(2,1)S(1)}, bf16[2,128,256]{2,1,0:T(8,128)(2,1)S(1)}, u32[]{:S(2)}, u32[]{:S(2)}) collective-permute-start(bf16[2,128,256]{2,1,0:T(8,128)(2,1)S(1)} %fusion.1), channel_id=1, source_target_pairs={{1,16},{3,18},{5,20},{7,22},{9,0},{11,2},{13,4},{15,6},{17,25},{19... | collective-permute-start | bytes 393224 | tf_op jit(solution)/shard_map/ppermute | solution.py:483
  147.1 15.3 %collective-permute-start.31 = (bf16[1,2,128,256]{3,2,1,0:T(8,128)(2,1)S(1)}, bf16[1,2,128,256]{3,2,1,0:T(8,128)(2,1)S(1)}, u32[]{:S(2)}, u32[]{:S(2)}) collective-permute-start(bf16[1,2,128,256]{3,2,1,0:T(8,128)(2,1)S(1)} %project_block.19), channel_id=1, source_target_pairs={{0,1},{1,0},{2,3},{3,2},{4,5},{5,4},{6,7},{7,6},{8,9},{9,8},{10,11... | collective-permute-start | bytes 393224 | tf_op jit(solution)/shard_map/ppermute | solution.py:467
  150.7 41.7 %collective-permute-start.29 = (bf16[2,128,256]{2,1,0:T(8,128)(2,1)}, bf16[2,128,256]{2,1,0:T(8,128)(2,1)}, u32[]{:S(2)}, u32[]{:S(2)}) collective-permute-start(bf16[2,128,256]{2,1,0:T(8,128)(2,1)} %fusion.2), channel_id=1, source_target_pairs={{0,24},{2,26},{4,28},{6,30},{8,16},{10,18},{12,20},{14,22},{16,9},... | collective-permute-start | bytes 393224 | tf_op jit(solution)/shard_map/ppermute | solution.py:483
  151.9 41.1 %collective-permute-start.30 = (bf16[2,128,256]{2,1,0:T(8,128)(2,1)}, bf16[2,128,256]{2,1,0:T(8,128)(2,1)}, u32[]{:S(2)}, u32[]{:S(2)}) collective-permute-start(bf16[2,128,256]{2,1,0:T(8,128)(2,1)} %fusion.2), channel_id=1, source_target_pairs={{1,24},{3,26},{5,28},{7,30},{9,16},{11,18},{13,20},{15,22},{17,9},... | collective-permute-start | bytes 393224 | tf_op jit(solution)/shard_map/ppermute | solution.py:483
  163.1 37.0 %collective-permute-start.32 = (bf16[2,128,256]{2,1,0:T(8,128)(2,1)}, bf16[2,128,256]{2,1,0:T(8,128)(2,1)}, u32[]{:S(2)}, u32[]{:S(2)}) collective-permute-start(bf16[2,128,256]{2,1,0:T(8,128)(2,1)} %fusion.3), channel_id=1, source_target_pairs={{0,8},{2,10},{4,12},{6,14},{8,24},{10,26},{12,28},{14,30},{16,1},{... | collective-permute-start | bytes 393224 | tf_op jit(solution)/shard_map/ppermute | solution.py:483
  164.4 37.1 %collective-permute-start.33 = (bf16[2,128,256]{2,1,0:T(8,128)(2,1)}, bf16[2,128,256]{2,1,0:T(8,128)(2,1)}, u32[]{:S(2)}, u32[]{:S(2)}) collective-permute-start(bf16[2,128,256]{2,1,0:T(8,128)(2,1)} %fusion.3), channel_id=1, source_target_pairs={{1,8},{3,10},{5,12},{7,14},{9,24},{11,26},{13,28},{15,30},{17,1},{... | collective-permute-start | bytes 393224 | tf_op jit(solution)/shard_map/ppermute | solution.py:483
  170.5 11.0 %collective-permute-start.34 = (bf16[2,2,128,256]{3,2,1,0:T(8,128)(2,1)S(1)}, bf16[2,2,128,256]{3,2,1,0:T(8,128)(2,1)S(1)}, u32[]{:S(2)}, u32[]{:S(2)}) collective-permute-start(bf16[2,2,128,256]{3,2,1,0:T(8,128)(2,1)S(1)} %project_block.21), channel_id=1, source_target_pairs={{0,1},{1,0},{2,3},{3,2},{4,5},{5,4},{6,7},{7,6},{8,9},{9,8},{10,11... | collective-permute-start | bytes 786440 | tf_op jit(solution)/shard_map/ppermute | solution.py:467
  188.7 20.1 %collective-permute-start.35 = (bf16[2,128,256]{2,1,0:T(8,128)(2,1)S(1)}, bf16[2,128,256]{2,1,0:T(8,128)(2,1)S(1)}, u32[]{:S(2)}, u32[]{:S(2)}) collective-permute-start(bf16[2,128,256]{2,1,0:T(8,128)(2,1)S(1)} %get-tuple-element.60.refs_8_), channel_id=1, source_target_pairs={{16,17},{18,19},{20,21},{22,23},{24,25},{26,27},{28,29},{30,31},{1... | collective-permute-start | bytes 393224 | tf_op jit(solution)/shard_map/ppermute | solution.py:482
  192.4 17.6 %collective-permute-start.36 = (bf16[2,128,256]{2,1,0:T(8,128)(2,1)S(1)}, bf16[2,128,256]{2,1,0:T(8,128)(2,1)S(1)}, u32[]{:S(2)}, u32[]{:S(2)}) collective-permute-start(bf16[2,128,256]{2,1,0:T(8,128)(2,1)S(1)} %get-tuple-element.59), channel_id=1, source_target_pairs={{0,16},{2,18},{4,20},{6,22},{8,0},{10,2},{12,4},{14,6},{16,25},{18... | collective-permute-start | bytes 393224 | tf_op jit(solution)/shard_map/ppermute | solution.py:483
  193.1 19.6 %collective-permute-start.37 = (bf16[2,128,256]{2,1,0:T(8,128)(2,1)S(1)}, bf16[2,128,256]{2,1,0:T(8,128)(2,1)S(1)}, u32[]{:S(2)}, u32[]{:S(2)}) collective-permute-start(bf16[2,128,256]{2,1,0:T(8,128)(2,1)S(1)} %get-tuple-element.59), channel_id=1, source_target_pairs={{1,16},{3,18},{5,20},{7,22},{9,0},{11,2},{13,4},{15,6},{17,25},{19... | collective-permute-start | bytes 393224 | tf_op jit(solution)/shard_map/ppermute | solution.py:483
  200.1 12.5 %collective-permute-start.39 = (bf16[2,128,256]{2,1,0:T(8,128)(2,1)S(1)}, bf16[2,128,256]{2,1,0:T(8,128)(2,1)S(1)}, u32[]{:S(2)}, u32[]{:S(2)}) collective-permute-start(bf16[2,128,256]{2,1,0:T(8,128)(2,1)S(1)} %get-tuple-element.58), channel_id=1, source_target_pairs={{0,24},{2,26},{4,28},{6,30},{8,16},{10,18},{12,20},{14,22},{16,9},... | collective-permute-start | bytes 393224 | tf_op jit(solution)/shard_map/ppermute | solution.py:483
  201.5 11.2 %collective-permute-start.40 = (bf16[2,128,256]{2,1,0:T(8,128)(2,1)S(1)}, bf16[2,128,256]{2,1,0:T(8,128)(2,1)S(1)}, u32[]{:S(2)}, u32[]{:S(2)}) collective-permute-start(bf16[2,128,256]{2,1,0:T(8,128)(2,1)S(1)} %get-tuple-element.58), channel_id=1, source_target_pairs={{1,24},{3,26},{5,28},{7,30},{9,16},{11,18},{13,20},{15,22},{17,9},... | collective-permute-start | bytes 393224 | tf_op jit(solution)/shard_map/ppermute | solution.py:483
  (36 other events, 294.3 us)
Sparse Core Ops, SparseCore 0:
  8.9 111.7 all-gather.2
where the time goes:
time: 243 us; the launch traced here: 242 us
  starting transfers between devices  95.4 us (39%)
  Pallas kernels  74.1 us (30%)
  waiting for transfers between devices  51.8 us (21%)
  between operations  14.2 us (6%)
  local copies, waits for them, and re-layouts  5 us (2%)
    pallas_call x12, Pallas kernels, project(): pl.pallas_call(functools.partial(project_kernel, len(blocks)), in_specs=[...  38.3 us
    ppermute x12, starting transfers between devices, deliver(): return [lax.ppermute(summed, ('ctx', 'tp'), moves) for moves in pairs]  37.4 us
    ppermute x6, waiting for transfers between devices, ring(): return lax.ppermute(array, 'ctx', pairs)  21.5 us
    pallas_call x1, Pallas kernels, per_device(): pl.pallas_call(functools.partial(place_kernel, kept, slabs), in_specs=[sm...  17.7 us
    ppermute x6, starting transfers between devices, ring(): return lax.ppermute(array, 'ctx', pairs)  14.1 us
    ppermute x12, waiting for transfers between devices, deliver(): return [lax.ppermute(summed, ('ctx', 'tp'), moves) for moves in pairs]  13.6 us
    ppermute x10, starting transfers between devices, within_slab(): return lax.ppermute(array, 'ctx', [(i, i ^ mask) for i in range(ctx)])  12.9 us
    ppermute x3, starting transfers between devices, per_device(): lax.ppermute(slab_left, 'ctx', [(i, i + by * SLAB) for i in range(ctx - b...  8.67 us
  transfers between devices with their start and end apart: 44, of which 17 were waited for; matrix products, arithmetic and copies ran while one was open for 1% of the time, Pallas kernels for 23%

commit v1 on v0

--- a/solution.py
+++ b/solution.py
@@ -185,21 +185,21 @@
         out_ref[:, pl.ds(tile * LANES, LANES)] = out_rows[pl.ds(tile * pitch, tokens), :].astype(BF16)
 
 
-def project_kernel(count, here, *refs):
+def project_kernel(count, picks, here, *refs):
     out_ref, slots, sems = refs[-3:]
-    pieces, depth, share = slots.shape
+    depth, share = slots.shape[1:]
     blocks, sources = refs[: SIDE * count], refs[SIDE * count : -3]
     half = depth // SIDE
     columns = pl.ds(pl.multiple_of(here[0] * share, share), share)
     copies = []
-    for i in range(pieces):
-        if len(sources) == pieces:
-            source = sources[i].at[:, columns]
+    for i, (which, rank) in enumerate(picks):
+        if rank is None:
+            source = sources[which].at[:, columns]
         else:
-            source = sources[0].at[here[1 + i], :, columns]
+            source = sources[which].at[here[rank], :, columns]
         copies.append(pltpu.make_async_copy(source, slots.at[i], sems.at[i]))
         copies[-1].start()
-    for i in range(pieces):
+    for i in range(len(picks)):
         copies[i].wait()
         for j in range(count):
             total = None
@@ -215,10 +215,9 @@
 
 def place_kernel(kept, steps, here, *refs):
     per_pair = 2 * steps
-    sources, out_ref, sems = refs[: SIDE * per_pair], refs[-2], refs[-1]
+    sources, out_ref = refs[: SIDE * per_pair], refs[-1]
     share = sources[0].shape[2]
     tp_me, rank = here[0], here[1]
-    waits = []
     for slot in range(kept):
         step = here[2 + slot]
         for pair in range(SIDE):
@@ -227,18 +226,17 @@
                 piece = rank ^ (SIDE * pair + near)
                 for t in range(SIDE):
                     start = ((slot * SLAB + piece) * SIDE + t) * share
-                    target = out_ref.at[:, pl.ds(pl.multiple_of(start, share), share)]
-                    sem = sems.at[len(waits)]
+                    target = pl.ds(pl.multiple_of(start, share), share)
                     own = jnp.logical_and(step == 0, tp_me == t)
                     moved = jnp.logical_and(step == 0, tp_me != t)
                     choices = [(own, mine[0]), (moved, mine[1])]
                     choices += [(step == k, mine[2 * k + t]) for k in range(1, steps)]
                     for chosen, source in choices:
-                        copy = pltpu.make_async_copy(source.at[near], target, sem)
-                        pl.when(chosen)(copy.start)
-                    waits.append(copy)
-    for copy in waits:
-        copy.wait()
+                        index = near if source.shape[0] == SIDE else SIDE * pair + near
+
+                        @pl.when(chosen)
+                        def _(source=source, index=index, target=target):
+                            out_ref[:, target] = source[index]
 
 
 def ring_order(count):
@@ -321,6 +319,7 @@
     )
     rows = jnp.concatenate([decay_rates, residues, skip_gain[None]], axis=0)
     rows = jnp.stack([rows] + [from_slab(rows, by) for by in range(1, slabs)])
+    rows, halo = lax.optimization_barrier((rows, halo))
     rates = slab_all(rows)
 
     beside = within_slab(out_weight, 1)
@@ -330,7 +329,8 @@
         axis_index_groups=[list(range(z * SLAB, (z + 1) * SLAB)) for z in range(slabs)],
     )
 
-    limit = pltpu.CompilerParams(vmem_limit_bytes=16 * 1024 * 1024)
+    limit = pltpu.CompilerParams(vmem_limit_bytes=52 * 1024 * 1024)
+    light = pl.CostEstimate(flops=1, bytes_accessed=1, transcendentals=0)
     series_shape = jax.ShapeDtypeStruct((groups, tokens, SUBLANES, LANES), F32)
     state_shape = jax.ShapeDtypeStruct((groups, modes, owned), BF16)
     scratch_rows = pltpu.VMEM((SUBLANES * (tokens + SUBLANES), LANES), F32)
@@ -341,7 +341,7 @@
         (1, 2 * modes + 1, owned), lambda g, here: (lax.rem(g - here[0] + slabs, slabs), 0, 0)
     )
 
-    def grouped(kernel, name, in_specs, out_specs, out_shape, scratch, ops, groups=groups):
+    def grouped(kernel, name, in_specs, out_specs, out_shape, scratch, groups=groups):
         return pl.pallas_call(
             kernel,
             grid_spec=pltpu.PrefetchScalarGridSpec(
@@ -353,11 +353,7 @@
             ),
             out_shape=out_shape,
             compiler_params=limit,
-            cost_estimate=pl.CostEstimate(
-                flops=ops * tokens * GROUP * groups,
-                bytes_accessed=4 * tokens * GROUP * groups,
-                transcendentals=0,
-            ),
+            cost_estimate=light,
             name=name,
         )
 
@@ -372,7 +368,6 @@
         [series, series],
         [series_shape, series_shape],
         [pltpu.VMEM((3 * TAPS, SUBLANES, LANES), F32), scratch_rows, scratch_rows, scratch_rows],
-        20,
     )(here, features, halo, conv_weight)
 
     left = grouped(
@@ -382,7 +377,6 @@
         [state_spec] * SLAB,
         [state_shape] * SLAB,
         [wide],
-        2 * modes,
     )(here, u, *rates)
     left = [left[0]] + [within_slab(left[d], d) for d in range(1, SLAB)]
 
@@ -394,6 +388,7 @@
         out_specs=vmem,
         out_shape=state_shape,
         compiler_params=limit,
+        cost_estimate=light,
         name="slab_states",
     )(here, rows, *left)
     earlier = [
@@ -408,7 +403,6 @@
         series,
         series_shape,
         [wide],
-        4 * modes,
     )(here, u, *rates)
 
     incoming = pl.pallas_call(
@@ -417,6 +411,7 @@
         out_specs=[vmem] * SLAB,
         out_shape=[state_shape] * SLAB,
         compiler_params=limit,
+        cost_estimate=light,
         name="incoming_states",
     )(here, rows, *left, *earlier)
     incoming = [incoming[0]] + [within_slab(incoming[d], d) for d in range(1, SLAB)]
@@ -435,37 +430,32 @@
             pl.BlockSpec((tokens, GROUP), lambda g, here: (0, g)),
             jax.ShapeDtypeStruct((tokens, width // SIDE), BF16),
             [wide, scratch_rows],
-            2 * modes,
             count,
         )(here, query, local, *rates, *incoming)
 
-    def project(blocks, sources, share_index):
+    def project(blocks, sources, picks, share_index):
         scalars = jnp.stack([share_index, rank ^ 2, rank ^ 3]).astype(jnp.int32)
-        rows = len(blocks) * tokens
         return pl.pallas_call(
-            functools.partial(project_kernel, len(blocks)),
+            functools.partial(project_kernel, len(blocks), picks),
             in_specs=[smem]
             + [vmem] * (SIDE * len(blocks))
             + [pl.BlockSpec(memory_space=pltpu.HBM)] * len(sources),
             out_specs=vmem,
-            out_shape=jax.ShapeDtypeStruct((len(blocks), SIDE, tokens, share), BF16),
+            out_shape=jax.ShapeDtypeStruct((len(blocks), len(picks), tokens, share), BF16),
             scratch_shapes=[
-                pltpu.VMEM((SIDE, depth, share), BF16),
-                pltpu.SemaphoreType.DMA((SIDE,)),
+                pltpu.VMEM((len(picks), depth, share), BF16),
+                pltpu.SemaphoreType.DMA((len(picks),)),
             ],
-            compiler_params=pltpu.CompilerParams(vmem_limit_bytes=48 * 1024 * 1024),
-            cost_estimate=pl.CostEstimate(
-                flops=2 * rows * depth * SIDE * share,
-                bytes_accessed=2 * depth * (rows + SIDE * share),
-                transcendentals=0,
-            ),
+            compiler_params=limit,
+            cost_estimate=light,
             name="project_block",
         )(scalars, *[h for b in blocks for h in b], *sources)
 
-    def summed_over_tp(blocks, sources):
-        away = project(blocks, sources, 1 - tp_me)
+    def summed_over_tp(blocks, sources, picks, away=None):
+        if away is None:
+            away = project(blocks, sources, picks, 1 - tp_me)
         got = lax.ppermute(away, "tp", [(0, 1), (1, 0)])
-        mine = project(blocks, sources, tp_me)
+        mine = project(blocks, sources, picks, tp_me)
         return (mine.astype(F32) + got.astype(F32)).astype(BF16)
 
     half_of = [z * tp // slabs for z in range(slabs)]
@@ -482,23 +472,31 @@
             return [summed, lax.ppermute(summed, ("ctx", "tp"), moves)]
         return [lax.ppermute(summed, ("ctx", "tp"), moves) for moves in pairs]
 
+    near, far, both = (
+        ((0, None), (1, None)),
+        ((0, 1), (0, 2)),
+        ((0, None), (1, None), (2, 1), (2, 2)),
+    )
     blocks = [[gated_half(h) for h in range(SIDE)]]
     arrived = [[], []]
-    for step in range(slabs):
+    summed = None
+    for step in range(slabs - 1):
+        first, second = blocks[step]
         if step:
-            blocks[step], summed, arrived[0] = lax.optimization_barrier(
-                (blocks[step], summed, arrived[0])
-            )
+            second, summed, arrived[0] = lax.optimization_barrier((second, summed, arrived[0]))
             arrived[0] += deliver(summed, step - 1)
-        if step < slabs - 1:
-            blocks.append([ring(h) for h in blocks[step]])
-        summed = summed_over_tp([blocks[step]], [out_weight, beside])[0]
-    arrived[0] += deliver(summed, slabs - 1)
-    slab_weights, _ = lax.optimization_barrier((slab_weights, blocks[-1]))
-    for first in range(0, slabs, 2):
-        pair = summed_over_tp(blocks[first : first + 2], [slab_weights])
-        for offset in range(pair.shape[0]):
-            arrived[1] += deliver(pair[offset], first + offset)
+        blocks.append([ring(first), ring(second)])
+        summed = summed_over_tp([blocks[step]], [out_weight, beside], near)[0]
+    slab_weights, summed, arrived[0] = lax.optimization_barrier((slab_weights, summed, arrived[0]))
+    arrived[0] += deliver(summed, slabs - 2)
+    away = project(blocks[: slabs - 1], [slab_weights], far, 1 - tp_me)
+    _, blocks[-1] = lax.optimization_barrier((away, blocks[-1]))
+    batch = summed_over_tp(blocks[: slabs - 1], [slab_weights], far, away)
+    for step in range(slabs - 1):
+        arrived[1] += deliver(batch[step], step)
+    last = summed_over_tp(blocks[slabs - 1 :], [out_weight, beside, slab_weights], both)
+    last = deliver(last[0], slabs - 1)
+    arrived = [a + last for a in arrived]
 
     def place_of(z):
         return sum(jnp.where(z == k, place[k], 0) for k in range(slabs))
@@ -509,11 +507,11 @@
     ]
     return pl.pallas_call(
         functools.partial(place_kernel, kept, slabs),
-        in_specs=[smem] + [pl.BlockSpec(memory_space=pl.ANY)] * (SIDE * 2 * slabs),
-        out_specs=pl.BlockSpec(memory_space=pl.ANY),
+        in_specs=[smem] + [vmem] * (SIDE * 2 * slabs),
+        out_specs=vmem,
         out_shape=jax.ShapeDtypeStruct((tokens, width), BF16),
-        scratch_shapes=[pltpu.SemaphoreType.DMA((kept * SLAB * SIDE,))],
         compiler_params=limit,
+        cost_estimate=light,
         name="place_columns",
     )(jnp.stack([tp_me, rank, *steps]).astype(jnp.int32), *arrived[0], *arrived[1])
 

time: 243 us -> 218 us (0.90)
  the two profiles are of different devices: /device:TPU:4 before, /device:TPU:26 now
where the time goes in v1:
time: 218 us
  Pallas kernels  72.6 us (33%)
  starting transfers between devices  70 us (32%)
  waiting for transfers between devices  54.2 us (25%)
  between operations  14 us (6%)
  local copies, waits for them, and re-layouts  5.52 us (3%)
    pallas_call x10, Pallas kernels, project(): pl.pallas_call(functools.partial(project_kernel, len(blocks), picks), in_...  43.1 us
    ppermute x10, starting transfers between devices, deliver(): return [lax.ppermute(summed, ('ctx', 'tp'), moves) for moves in pairs]  25.8 us
    ppermute x6, waiting for transfers between devices, ring(): return lax.ppermute(array, 'ctx', pairs)  24.2 us
    ppermute x5, starting transfers between devices, summed_over_tp(): got = lax.ppermute(away, 'tp', [(0, 1), (1, 0)])  17.3 us
    ppermute x10, waiting for transfers between devices, within_slab(): return lax.ppermute(array, 'ctx', [(i, i ^ mask) for i in range(ctx)])  10.1 us
    ppermute x10, waiting for transfers between devices, deliver(): return [lax.ppermute(summed, ('ctx', 'tp'), moves) for moves in pairs]  8.14 us
    ppermute x3, waiting for transfers between devices, per_device(): lax.ppermute(slab_left, 'ctx', [(i, i + by * SLAB) for i in range(ctx - b...  7.69 us
    pallas_call x1, Pallas kernels, per_device(): grouped(functools.partial(local_kernel, modes), 'local_convolution', [ser...  7.45 us
  transfers between devices with their start and end apart: 41, of which 15 were waited for; matrix products, arithmetic and copies ran while one was open for 1% of the time, Pallas kernels for 32%

profile of v1, /device:TPU:26, one launch (start us, length us, event | category | flops | bytes accessed | tf_op | source)
XLA Modules:
  0.0 217.5 jit_solution(10100880259733529625)
XLA Ops:
  19.6 6.5 %short_filters.1 = (f32[4,128,8,128]{3,2,1,0:T(8,128)}, f32[4,128,8,128]{3,2,1,0:T(8,128)}) custom-call(s32[3]{0:T(128)S(1)} %pad_add_fusion.1.here, bf16[3,128,4096]{2,1,0:T(8,128)(2,1)} %features.1, bf16[3,2,4096]{2,1,0:T(2,128)(2,1)S(1)} %collective-permute-done.3.halo, f32[3,3,8192]{2,1,0:T(4,128)S(1)} %copy-done.3), custom_call_target="tpu_custom_call" | custom-call | flops 1 | bytes 1 | tf_op jit(solution)/shard_map/short_filters/pallas_call | solution.py:360
  26.3 5.6 %collective-permute-done.6.refs_3_ = f32[4,33,256]{2,1,0:T(8,128)S(1)} collective-permute-done((f32[4,33,256]{2,1,0:T(8,128)S(1)}, f32[4,33,256]{2,1,0:T(8,128)S(1)}, u32[]{:S(2)}, u32[]{:S(2)}) %collective-permute-start.6) | collective-permute-done | bytes 135200 | tf_op jit(solution)/shard_map/ppermute | solution.py:302
  31.9 4.6 %block_states.1 = (bf16[4,16,256]{2,1,0:T(8,128)(2,1)S(1)}, bf16[4,16,256]{2,1,0:T(8,128)(2,1)S(1)}, bf16[4,16,256]{2,1,0:T(8,128)(2,1)S(1)}, bf16[4,16,256]{2,1,0:T(8,128)(2,1)S(1)}) custom-call(s32[3]{0:T(128)S(1)} %pad_add_fusion.1.here, f32[4,128,8,128]{3,2,1,0:T(8,128)} %get-tuple-element.33.u_ref, f32[4,33,256]{2,1,0:T(8,128)S(1)} %pad_maximum_fusion.refs_0_.rates, ...), custom_call_target="tpu_custom_call" | custom-call | flops 1 | bytes 1 | tf_op jit(solution)/shard_map/block_states/pallas_call | solution.py:373
  58.5 7.4 %local_convolution.1.y_ref = f32[4,128,8,128]{3,2,1,0:T(8,128)} custom-call(s32[3]{0:T(128)S(1)} %pad_add_fusion.1.here, f32[4,128,8,128]{3,2,1,0:T(8,128)} %get-tuple-element.33.u_ref, f32[4,33,256]{2,1,0:T(8,128)S(1)} %pad_maximum_fusion.refs_0_.rates, f32[4,33,256]{2,1,0:T(8,128)S(1)} %collective-permute-done.4.refs_1_, ...), custom_call_target="tpu_custom_call" | custom-call | flops 1 | bytes 1 | tf_op jit(solution)/shard_map/local_convolution/pallas_call | solution.py:399
  66.0 3.6 %gated_block.2.refs_0_ = bf16[128,2048]{1,0:T(8,128)(2,1)S(1)} custom-call(s32[3]{0:T(128)S(1)} %pad_add_fusion.1.here, f32[4,128,8,128]{3,2,1,0:T(8,128)} %get-tuple-element.32.query_ref, f32[4,128,8,128]{3,2,1,0:T(8,128)} %local_convolution.1.y_ref, f32[4,33,256]{2,1,0:T(8,128)S(1)} %pad_maximum_fusion.refs_0_.rates, ...), custom_call_target="tpu_custom_call" | custom-call | flops 1 | bytes 1 | tf_op jit(solution)/shard_map/gated_block/pallas_call | solution.py:426
  69.6 3.6 %gated_block.3.refs_1_ = bf16[128,2048]{1,0:T(8,128)(2,1)S(1)} custom-call(s32[3]{0:T(128)S(1)} %pad_add_fusion.1.here, f32[4,128,8,128]{3,2,1,0:T(8,128)} %get-tuple-element.32.query_ref, f32[4,128,8,128]{3,2,1,0:T(8,128)} %local_convolution.1.y_ref, f32[4,33,256]{2,1,0:T(8,128)S(1)} %pad_maximum_fusion.refs_0_.rates, ...), custom_call_target="tpu_custom_call" | custom-call | flops 1 | bytes 1 | tf_op jit(solution)/shard_map/gated_block/pallas_call | solution.py:426
  73.7 3.5 %project_block.11 = bf16[1,2,128,256]{3,2,1,0:T(8,128)(2,1)S(1)} custom-call(s32[3]{0:T(128)S(1)} %add_add_fusion.1.here, bf16[128,2048]{1,0:T(8,128)(2,1)S(1)} %gated_block.2.refs_0_, bf16[128,2048]{1,0:T(8,128)(2,1)S(1)} %gated_block.3.refs_1_, bf16[4096,512]{1,0:T(8,128)(2,1)} %refs_2_.15, bf16[4096,512]{1,0:T(8,128)(2,1)} %collective-permute-done.19.refs_3_), custom_call_target="tpu_custom_call" | custom-call | flops 1 | bytes 1 | tf_op jit(solution)/shard_map/project_block/pallas_call | solution.py:438
  78.9 6.3 %collective-permute-done.16.refs_0_.refs_2_ = bf16[128,2048]{1,0:T(8,128)(2,1)S(1)} collective-permute-done((bf16[128,2048]{1,0:T(8,128)(2,1)S(1)}, bf16[128,2048]{1,0:T(8,128)(2,1)S(1)}, u32[]{:S(2)}, u32[]{:S(2)}) %collective-permute-start.16) | collective-permute-done | bytes 524320 | tf_op jit(solution)/shard_map/ppermute | solution.py:315
  85.3 3.5 %project_block.10 = bf16[1,2,128,256]{3,2,1,0:T(8,128)(2,1)S(1)} custom-call(s32[3]{0:T(128)S(1)} %add_add_fusion.here, bf16[128,2048]{1,0:T(8,128)(2,1)S(1)} %gated_block.2.refs_0_, bf16[128,2048]{1,0:T(8,128)(2,1)S(1)} %gated_block.3.refs_1_, bf16[4096,512]{1,0:T(8,128)(2,1)} %refs_2_.15, bf16[4096,512]{1,0:T(8,128)(2,1)} %collective-permute-done.19.refs_3_), custom_call_target="tpu_custom_call" | custom-call | flops 1 | bytes 1 | tf_op jit(solution)/shard_map/project_block/pallas_call | solution.py:438
  88.9 7.6 %collective-permute-done.18.refs_1_.refs_3_ = bf16[128,2048]{1,0:T(8,128)(2,1)S(1)} collective-permute-done((bf16[128,2048]{1,0:T(8,128)(2,1)S(1)}, bf16[128,2048]{1,0:T(8,128)(2,1)S(1)}, u32[]{:S(2)}, u32[]{:S(2)}) %collective-permute-start.18) | collective-permute-done | bytes 524320 | tf_op jit(solution)/shard_map/ppermute | solution.py:315
  96.5 3.5 %project_block.15 = bf16[1,2,128,256]{3,2,1,0:T(8,128)(2,1)S(1)} custom-call(s32[3]{0:T(128)S(1)} %add_add_fusion.1.here, bf16[128,2048]{1,0:T(8,128)(2,1)S(1)} %collective-permute-done.16.refs_0_.refs_2_, bf16[128,2048]{1,0:T(8,128)(2,1)S(1)} %collective-permute-done.18.refs_1_.refs_3_, bf16[4096,512]{1,0:T(8,128)(2,1)} %refs_2_.15, ...), custom_call_target="tpu_custom_call" | custom-call | flops 1 | bytes 1 | tf_op jit(solution)/shard_map/project_block/pallas_call | solution.py:438
  101.7 6.0 %collective-permute-done.17.refs_0_.refs_4_ = bf16[128,2048]{1,0:T(8,128)(2,1)S(1)} collective-permute-done((bf16[128,2048]{1,0:T(8,128)(2,1)S(1)}, bf16[128,2048]{1,0:T(8,128)(2,1)S(1)}, u32[]{:S(2)}, u32[]{:S(2)}) %collective-permute-start.17) | collective-permute-done | bytes 524320 | tf_op jit(solution)/shard_map/ppermute | solution.py:315
  107.7 3.5 %project_block.14 = bf16[1,2,128,256]{3,2,1,0:T(8,128)(2,1)S(1)} custom-call(s32[3]{0:T(128)S(1)} %add_add_fusion.here, bf16[128,2048]{1,0:T(8,128)(2,1)S(1)} %collective-permute-done.16.refs_0_.refs_2_, bf16[128,2048]{1,0:T(8,128)(2,1)S(1)} %collective-permute-done.18.refs_1_.refs_3_, bf16[4096,512]{1,0:T(8,128)(2,1)} %refs_2_.15, ...), custom_call_target="tpu_custom_call" | custom-call | flops 1 | bytes 1 | tf_op jit(solution)/shard_map/project_block/pallas_call | solution.py:438
  114.8 4.2 %collective-permute-done.21.refs_1_.refs_5_ = bf16[128,2048]{1,0:T(8,128)(2,1)S(1)} collective-permute-done((bf16[128,2048]{1,0:T(8,128)(2,1)S(1)}, bf16[128,2048]{1,0:T(8,128)(2,1)S(1)}, u32[]{:S(2)}, u32[]{:S(2)}) %collective-permute-start.21) | collective-permute-done | bytes 524320 | tf_op jit(solution)/shard_map/ppermute | solution.py:315
  119.0 3.5 %project_block.13 = bf16[1,2,128,256]{3,2,1,0:T(8,128)(2,1)S(1)} custom-call(s32[3]{0:T(128)S(1)} %add_add_fusion.1.here, bf16[128,2048]{1,0:T(8,128)(2,1)S(1)} %collective-permute-done.17.refs_0_.refs_4_, bf16[128,2048]{1,0:T(8,128)(2,1)S(1)} %collective-permute-done.21.refs_1_.refs_5_, bf16[4096,512]{1,0:T(8,128)(2,1)} %refs_2_.15, ...), custom_call_target="tpu_custom_call" | custom-call | flops 1 | bytes 1 | tf_op jit(solution)/shard_map/project_block/pallas_call | solution.py:438
  129.4 3.5 %project_block.12 = bf16[1,2,128,256]{3,2,1,0:T(8,128)(2,1)S(1)} custom-call(s32[3]{0:T(128)S(1)} %add_add_fusion.here, bf16[128,2048]{1,0:T(8,128)(2,1)S(1)} %collective-permute-done.17.refs_0_.refs_4_, bf16[128,2048]{1,0:T(8,128)(2,1)S(1)} %collective-permute-done.21.refs_1_.refs_5_, bf16[4096,512]{1,0:T(8,128)(2,1)} %refs_2_.15, ...), custom_call_target="tpu_custom_call" | custom-call | flops 1 | bytes 1 | tf_op jit(solution)/shard_map/project_block/pallas_call | solution.py:438
  134.3 5.5 %project_block.16 = bf16[3,2,128,256]{3,2,1,0:T(8,128)(2,1)S(1)} custom-call(s32[3]{0:T(128)S(1)} %add_add_fusion.1.here, bf16[128,2048]{1,0:T(8,128)(2,1)S(1)} %gated_block.2.refs_0_, bf16[128,2048]{1,0:T(8,128)(2,1)S(1)} %gated_block.3.refs_1_, bf16[128,2048]{1,0:T(8,128)(2,1)S(1)} %collective-permute-done.16.refs_0_.refs_2_, bf16[128,2048]{1,0:T(8,128)(2,1)} %copy-done, ...), custom_call_target="tpu_custom_call" | custom-call | flops 1 | bytes 1 | tf_op jit(solution)/shard_map/project_block/pallas_call | solution.py:438
  139.8 11.7 %collective-permute-start.34 = (bf16[3,2,128,256]{3,2,1,0:T(8,128)(2,1)S(1)}, bf16[3,2,128,256]{3,2,1,0:T(8,128)(2,1)S(1)}, u32[]{:S(2)}, u32[]{:S(2)}) collective-permute-start(bf16[3,2,128,256]{3,2,1,0:T(8,128)(2,1)S(1)} %project_block.16), channel_id=1, source_target_pairs={{0,1},{1,0},{2,3},{3,2},{4,5},{5,4},{6,7},{7,6},{8,9},{9,8},{10,11... | collective-permute-start | bytes 1179656 | tf_op jit(solution)/shard_map/ppermute | solution.py:457
  151.6 4.8 %collective-permute-start.27 = (bf16[2,128,256]{2,1,0:T(8,128)(2,1)S(1)}, bf16[2,128,256]{2,1,0:T(8,128)(2,1)S(1)}, u32[]{:S(2)}, u32[]{:S(2)}) collective-permute-start(bf16[2,128,256]{2,1,0:T(8,128)(2,1)S(1)} %copy-done.11), channel_id=1, source_target_pairs={{0,24},{2,26},{4,28},{6,30},{8,16},{10,18},{12,20},{14,22},{16,9},... | collective-permute-start | bytes 393224 | tf_op jit(solution)/shard_map/ppermute | solution.py:473
  157.9 5.4 %project_block.18 = bf16[1,4,128,256]{3,2,1,0:T(8,128)(2,1)S(1)} custom-call(s32[3]{0:T(128)S(1)} %add_add_fusion.1.here, bf16[128,2048]{1,0:T(8,128)(2,1)} %collective-permute-done.29.refs_0_, bf16[128,2048]{1,0:T(8,128)(2,1)S(1)} %collective-permute-done.30.refs_1_, bf16[4096,512]{1,0:T(8,128)(2,1)} %refs_2_.15, ...), custom_call_target="tpu_custom_call" | custom-call | flops 1 | bytes 1 | tf_op jit(solution)/shard_map/project_block/pallas_call | solution.py:438
  164.0 5.5 %project_block.19 = bf16[3,2,128,256]{3,2,1,0:T(8,128)(2,1)S(1)} custom-call(s32[3]{0:T(128)S(1)} %add_add_fusion.here, bf16[128,2048]{1,0:T(8,128)(2,1)S(1)} %gated_block.2.refs_0_, bf16[128,2048]{1,0:T(8,128)(2,1)S(1)} %gated_block.3.refs_1_, bf16[128,2048]{1,0:T(8,128)(2,1)S(1)} %collective-permute-done.16.refs_0_.refs_2_, bf16[128,2048]{1,0:T(8,128)(2,1)} %copy-done, ...), custom_call_target="tpu_custom_call" | custom-call | flops 1 | bytes 1 | tf_op jit(solution)/shard_map/project_block/pallas_call | solution.py:438
  169.5 5.5 %project_block.17 = bf16[1,4,128,256]{3,2,1,0:T(8,128)(2,1)S(1)} custom-call(s32[3]{0:T(128)S(1)} %add_add_fusion.here, bf16[128,2048]{1,0:T(8,128)(2,1)} %collective-permute-done.29.refs_0_, bf16[128,2048]{1,0:T(8,128)(2,1)S(1)} %collective-permute-done.30.refs_1_, bf16[4096,512]{1,0:T(8,128)(2,1)} %refs_2_.15, ...), custom_call_target="tpu_custom_call" | custom-call | flops 1 | bytes 1 | tf_op jit(solution)/shard_map/project_block/pallas_call | solution.py:438
  185.1 11.1 %collective-permute-start.38 = (bf16[2,128,256]{2,1,0:T(8,128)(2,1)S(1)}, bf16[2,128,256]{2,1,0:T(8,128)(2,1)S(1)}, u32[]{:S(2)}, u32[]{:S(2)}) collective-permute-start(bf16[2,128,256]{2,1,0:T(8,128)(2,1)S(1)} %get-tuple-element.57), channel_id=1, source_target_pairs={{0,24},{2,26},{4,28},{6,30},{8,16},{10,18},{12,20},{14,22},{16,9},... | collective-permute-start | bytes 393224 | tf_op jit(solution)/shard_map/ppermute | solution.py:473
  198.7 7.1 %collective-permute-done.39.refs_13_ = bf16[2,128,256]{2,1,0:T(8,128)(2,1)S(1)} collective-permute-done((bf16[2,128,256]{2,1,0:T(8,128)(2,1)S(1)}, bf16[2,128,256]{2,1,0:T(8,128)(2,1)S(1)}, u32[]{:S(2)}, u32[]{:S(2)}) %collective-permute-start.39) | collective-permute-done | bytes 131104 | tf_op jit(solution)/shard_map/ppermute | solution.py:473
  (120 shorter events, 70.3 us)
Async XLA Ops:
  6.5 127.7 %all-gather.3.cloned.1.call-start = ((), (), s32[]{:S(2)}) async-start(), calls=%async_computation | async-start | bytes 20971520 | tf_op jit(solution)/shard_map/all_gather | solution.py:326
  7.3 66.4 %collective-permute-start.19 = (bf16[4096,512]{1,0:T(8,128)(2,1)}, bf16[4096,512]{1,0:T(8,128)(2,1)}, u32[]{:S(2)}, u32[]{:S(2)}) collective-permute-start(bf16[4096,512]{1,0:T(8,128)(2,1)} %refs_2_.15), channel_id=1, source_target_pairs={{0,2},{2,0},{4,6},{6,4},{8,10},{10,8},{12,14},{14,12},{16,18},{18,... | collective-permute-start | bytes 12582920 | tf_op jit(solution)/shard_map/ppermute | solution.py:302
  19.1 12.8 %collective-permute-start.6 = (f32[4,33,256]{2,1,0:T(8,128)S(1)}, f32[4,33,256]{2,1,0:T(8,128)S(1)}, u32[]{:S(2)}, u32[]{:S(2)}) collective-permute-start(f32[4,33,256]{2,1,0:T(8,128)S(1)} %pad_maximum_fusion.refs_0_.rates), channel_id=1, source_target_pairs={{0,6},{2,4},{4,2},{6,0},{8,14},{10,12},{12,10},{14,8},{16,22},{18,... | collective-permute-start | bytes 405512 | tf_op jit(solution)/shard_map/ppermute | solution.py:302
  69.6 15.7 %collective-permute-start.16 = (bf16[128,2048]{1,0:T(8,128)(2,1)S(1)}, bf16[128,2048]{1,0:T(8,128)(2,1)S(1)}, u32[]{:S(2)}, u32[]{:S(2)}) collective-permute-start(bf16[128,2048]{1,0:T(8,128)(2,1)S(1)} %gated_block.2.refs_0_), channel_id=1, source_target_pairs={{0,8},{2,10},{4,12},{6,14},{8,24},{10,26},{12,28},{14,30},{16,0},{... | collective-permute-start | bytes 1572872 | tf_op jit(solution)/shard_map/ppermute | solution.py:315
  73.2 23.3 %collective-permute-start.18 = (bf16[128,2048]{1,0:T(8,128)(2,1)S(1)}, bf16[128,2048]{1,0:T(8,128)(2,1)S(1)}, u32[]{:S(2)}, u32[]{:S(2)}) collective-permute-start(bf16[128,2048]{1,0:T(8,128)(2,1)S(1)} %gated_block.3.refs_1_), channel_id=1, source_target_pairs={{0,8},{2,10},{4,12},{6,14},{8,24},{10,26},{12,28},{14,30},{16,0},{... | collective-permute-start | bytes 1572872 | tf_op jit(solution)/shard_map/ppermute | solution.py:315
  77.2 11.6 %collective-permute-start.20 = (bf16[1,2,128,256]{3,2,1,0:T(8,128)(2,1)S(1)}, bf16[1,2,128,256]{3,2,1,0:T(8,128)(2,1)S(1)}, u32[]{:S(2)}, u32[]{:S(2)}) collective-permute-start(bf16[1,2,128,256]{3,2,1,0:T(8,128)(2,1)S(1)} %project_block.11), channel_id=1, source_target_pairs={{0,1},{1,0},{2,3},{3,2},{4,5},{5,4},{6,7},{7,6},{8,9},{9,8},{10,11... | collective-permute-start | bytes 393224 | tf_op jit(solution)/shard_map/ppermute | solution.py:457
  85.3 22.5 %collective-permute-start.17 = (bf16[128,2048]{1,0:T(8,128)(2,1)S(1)}, bf16[128,2048]{1,0:T(8,128)(2,1)S(1)}, u32[]{:S(2)}, u32[]{:S(2)}) collective-permute-start(bf16[128,2048]{1,0:T(8,128)(2,1)S(1)} %collective-permute-done.16.refs_0_.refs_2_), channel_id=1, source_target_pairs={{0,8},{2,10},{4,12},{6,14},{8,24},{10,26},{12,28},{14,30},{16,0},{... | collective-permute-start | bytes 1572872 | tf_op jit(solution)/shard_map/ppermute | solution.py:315
  96.5 22.5 %collective-permute-start.21 = (bf16[128,2048]{1,0:T(8,128)(2,1)S(1)}, bf16[128,2048]{1,0:T(8,128)(2,1)S(1)}, u32[]{:S(2)}, u32[]{:S(2)}) collective-permute-start(bf16[128,2048]{1,0:T(8,128)(2,1)S(1)} %collective-permute-done.18.refs_1_.refs_3_), channel_id=1, source_target_pairs={{0,8},{2,10},{4,12},{6,14},{8,24},{10,26},{12,28},{14,30},{16,0},{... | collective-permute-start | bytes 1572872 | tf_op jit(solution)/shard_map/ppermute | solution.py:315
  100.0 24.1 %collective-permute-start.23 = (bf16[1,2,128,256]{3,2,1,0:T(8,128)(2,1)S(1)}, bf16[1,2,128,256]{3,2,1,0:T(8,128)(2,1)S(1)}, u32[]{:S(2)}, u32[]{:S(2)}) collective-permute-start(bf16[1,2,128,256]{3,2,1,0:T(8,128)(2,1)S(1)} %project_block.15), channel_id=1, source_target_pairs={{0,1},{1,0},{2,3},{3,2},{4,5},{5,4},{6,7},{7,6},{8,9},{9,8},{10,11... | collective-permute-start | bytes 393224 | tf_op jit(solution)/shard_map/ppermute | solution.py:457
  107.7 50.1 %collective-permute-start.29 = (bf16[128,2048]{1,0:T(8,128)(2,1)S(1)}, bf16[128,2048]{1,0:T(8,128)(2,1)}, u32[]{:S(2)}, u32[]{:S(2)}) collective-permute-start(bf16[128,2048]{1,0:T(8,128)(2,1)S(1)} %collective-permute-done.17.refs_0_.refs_4_), channel_id=1, source_target_pairs={{0,8},{2,10},{4,12},{6,14},{8,24},{10,26},{12,28},{14,30},{16,0},{... | collective-permute-start | bytes 1572872 | tf_op jit(solution)/shard_map/ppermute | solution.py:315
  111.3 12.9 %collective-permute-start.24 = (bf16[2,128,256]{2,1,0:T(8,128)(2,1)S(1)}, bf16[2,128,256]{2,1,0:T(8,128)(2,1)S(1)}, u32[]{:S(2)}, u32[]{:S(2)}) collective-permute-start(bf16[2,128,256]{2,1,0:T(8,128)(2,1)S(1)} %fusion.1.refs_0_), channel_id=1, source_target_pairs={{16,17},{18,19},{20,21},{22,23},{24,25},{26,27},{28,29},{30,31},{1... | collective-permute-start | bytes 393224 | tf_op jit(solution)/shard_map/ppermute | solution.py:472
  122.5 10.4 %collective-permute-start.22 = (bf16[1,2,128,256]{3,2,1,0:T(8,128)(2,1)S(1)}, bf16[1,2,128,256]{3,2,1,0:T(8,128)(2,1)S(1)}, u32[]{:S(2)}, u32[]{:S(2)}) collective-permute-start(bf16[1,2,128,256]{3,2,1,0:T(8,128)(2,1)S(1)} %project_block.13), channel_id=1, source_target_pairs={{0,1},{1,0},{2,3},{3,2},{4,5},{5,4},{6,7},{7,6},{8,9},{9,8},{10,11... | collective-permute-start | bytes 393224 | tf_op jit(solution)/shard_map/ppermute | solution.py:457
  126.2 31.7 %collective-permute-start.30 = (bf16[128,2048]{1,0:T(8,128)(2,1)S(1)}, bf16[128,2048]{1,0:T(8,128)(2,1)S(1)}, u32[]{:S(2)}, u32[]{:S(2)}) collective-permute-start(bf16[128,2048]{1,0:T(8,128)(2,1)S(1)} %collective-permute-done.21.refs_1_.refs_5_), channel_id=1, source_target_pairs={{0,8},{2,10},{4,12},{6,14},{8,24},{10,26},{12,28},{14,30},{16,0},{... | collective-permute-start | bytes 1572872 | tf_op jit(solution)/shard_map/ppermute | solution.py:315
  139.8 35.1 %collective-permute-start.34 = (bf16[3,2,128,256]{3,2,1,0:T(8,128)(2,1)S(1)}, bf16[3,2,128,256]{3,2,1,0:T(8,128)(2,1)S(1)}, u32[]{:S(2)}, u32[]{:S(2)}) collective-permute-start(bf16[3,2,128,256]{3,2,1,0:T(8,128)(2,1)S(1)} %project_block.16), channel_id=1, source_target_pairs={{0,1},{1,0},{2,3},{3,2},{4,5},{5,4},{6,7},{7,6},{8,9},{9,8},{10,11... | collective-permute-start | bytes 1179656 | tf_op jit(solution)/shard_map/ppermute | solution.py:457
  151.6 30.3 %collective-permute-start.27 = (bf16[2,128,256]{2,1,0:T(8,128)(2,1)S(1)}, bf16[2,128,256]{2,1,0:T(8,128)(2,1)S(1)}, u32[]{:S(2)}, u32[]{:S(2)}) collective-permute-start(bf16[2,128,256]{2,1,0:T(8,128)(2,1)S(1)} %copy-done.11), channel_id=1, source_target_pairs={{0,24},{2,26},{4,28},{6,30},{8,16},{10,18},{12,20},{14,22},{16,9},... | collective-permute-start | bytes 393224 | tf_op jit(solution)/shard_map/ppermute | solution.py:473
  156.4 27.4 %collective-permute-start.28 = (bf16[2,128,256]{2,1,0:T(8,128)(2,1)S(1)}, bf16[2,128,256]{2,1,0:T(8,128)(2,1)S(1)}, u32[]{:S(2)}, u32[]{:S(2)}) collective-permute-start(bf16[2,128,256]{2,1,0:T(8,128)(2,1)S(1)} %copy-done.11), channel_id=1, source_target_pairs={{1,24},{3,26},{5,28},{7,30},{9,16},{11,18},{13,20},{15,22},{17,9},... | collective-permute-start | bytes 393224 | tf_op jit(solution)/shard_map/ppermute | solution.py:473
  163.3 15.2 %collective-permute-start.31 = (bf16[1,4,128,256]{3,2,1,0:T(8,128)(2,1)S(1)}, bf16[1,4,128,256]{3,2,1,0:T(8,128)(2,1)S(1)}, u32[]{:S(2)}, u32[]{:S(2)}) collective-permute-start(bf16[1,4,128,256]{3,2,1,0:T(8,128)(2,1)S(1)} %project_block.18), channel_id=1, source_target_pairs={{0,1},{1,0},{2,3},{3,2},{4,5},{5,4},{6,7},{7,6},{8,9},{9,8},{10,11... | collective-permute-start | bytes 786440 | tf_op jit(solution)/shard_map/ppermute | solution.py:457
  175.1 10.0 %collective-permute-start.35 = (bf16[2,128,256]{2,1,0:T(8,128)(2,1)S(1)}, bf16[2,128,256]{2,1,0:T(8,128)(2,1)S(1)}, u32[]{:S(2)}, u32[]{:S(2)}) collective-permute-start(bf16[2,128,256]{2,1,0:T(8,128)(2,1)S(1)} %get-tuple-element.59.refs_8_), channel_id=1, source_target_pairs={{16,17},{18,19},{20,21},{22,23},{24,25},{26,27},{28,29},{30,31},{1... | collective-permute-start | bytes 393224 | tf_op jit(solution)/shard_map/ppermute | solution.py:472
  178.6 17.6 %collective-permute-start.36 = (bf16[2,128,256]{2,1,0:T(8,128)(2,1)S(1)}, bf16[2,128,256]{2,1,0:T(8,128)(2,1)S(1)}, u32[]{:S(2)}, u32[]{:S(2)}) collective-permute-start(bf16[2,128,256]{2,1,0:T(8,128)(2,1)S(1)} %get-tuple-element.58), channel_id=1, source_target_pairs={{0,16},{2,18},{4,20},{6,22},{8,0},{10,2},{12,4},{14,6},{16,25},{18... | collective-permute-start | bytes 393224 | tf_op jit(solution)/shard_map/ppermute | solution.py:473
  179.9 25.9 %collective-permute-start.32 = (bf16[4,128,256]{2,1,0:T(8,128)(2,1)S(1)}, bf16[4,128,256]{2,1,0:T(8,128)(2,1)S(1)}, u32[]{:S(2)}, u32[]{:S(2)}) collective-permute-start(bf16[4,128,256]{2,1,0:T(8,128)(2,1)S(1)} %fusion), channel_id=1, source_target_pairs={{0,8},{2,10},{4,12},{6,14},{8,24},{10,26},{12,28},{14,30},{16,1},{... | collective-permute-start | bytes 786440 | tf_op jit(solution)/shard_map/ppermute | solution.py:473
  182.5 23.3 %collective-permute-start.33 = (bf16[4,128,256]{2,1,0:T(8,128)(2,1)S(1)}, bf16[4,128,256]{2,1,0:T(8,128)(2,1)S(1)}, u32[]{:S(2)}, u32[]{:S(2)}) collective-permute-start(bf16[4,128,256]{2,1,0:T(8,128)(2,1)S(1)} %fusion), channel_id=1, source_target_pairs={{1,8},{3,10},{5,12},{7,14},{9,24},{11,26},{13,28},{15,30},{17,1},{... | collective-permute-start | bytes 786440 | tf_op jit(solution)/shard_map/ppermute | solution.py:473
  184.4 13.2 %collective-permute-start.37 = (bf16[2,128,256]{2,1,0:T(8,128)(2,1)S(1)}, bf16[2,128,256]{2,1,0:T(8,128)(2,1)S(1)}, u32[]{:S(2)}, u32[]{:S(2)}) collective-permute-start(bf16[2,128,256]{2,1,0:T(8,128)(2,1)S(1)} %get-tuple-element.58), channel_id=1, source_target_pairs={{1,16},{3,18},{5,20},{7,22},{9,0},{11,2},{13,4},{15,6},{17,25},{19... | collective-permute-start | bytes 393224 | tf_op jit(solution)/shard_map/ppermute | solution.py:473
  185.1 13.6 %collective-permute-start.38 = (bf16[2,128,256]{2,1,0:T(8,128)(2,1)S(1)}, bf16[2,128,256]{2,1,0:T(8,128)(2,1)S(1)}, u32[]{:S(2)}, u32[]{:S(2)}) collective-permute-start(bf16[2,128,256]{2,1,0:T(8,128)(2,1)S(1)} %get-tuple-element.57), channel_id=1, source_target_pairs={{0,24},{2,26},{4,28},{6,30},{8,16},{10,18},{12,20},{14,22},{16,9},... | collective-permute-start | bytes 393224 | tf_op jit(solution)/shard_map/ppermute | solution.py:473
  196.2 9.6 %collective-permute-start.39 = (bf16[2,128,256]{2,1,0:T(8,128)(2,1)S(1)}, bf16[2,128,256]{2,1,0:T(8,128)(2,1)S(1)}, u32[]{:S(2)}, u32[]{:S(2)}) collective-permute-start(bf16[2,128,256]{2,1,0:T(8,128)(2,1)S(1)} %get-tuple-element.57), channel_id=1, source_target_pairs={{1,24},{3,26},{5,28},{7,30},{9,16},{11,18},{13,20},{15,22},{17,9},... | collective-permute-start | bytes 393224 | tf_op jit(solution)/shard_map/ppermute | solution.py:473
  (32 other events, 239.4 us)
Sparse Core Ops, SparseCore 0:
  8.9 113.6 all-gather.2
